TPU v7x, 128 devices: a whole 4x4x4 slice. The times are simulated.
128 devices in a mesh: pos: 32 (over x, z, core), diag: 4 (over y).
Axes of the slice: x: 4, y: 4, z: 4, core: 2. Of those that a mesh axis runs over, the one named last changes fastest.
Arguments:
- bin_features: bfloat16 [12288, 256], P(('pos', 'diag')), may hold values from -6 to 6
- left_weight: bfloat16 [256, 64], replicated, may hold values from -0.375 to 0.375
- right_weight: bfloat16 [256, 64], replicated, may hold values from -0.375 to 0.375
- kernel_one: bfloat16 [9, 64, 64], replicated, may hold values from -0.25 to 0.25
- kernel_two: bfloat16 [9, 64, 64], replicated, may hold values from -0.25 to 0.25
- out_weight: bfloat16 [64], replicated, may hold values from -0.75 to 0.75
- dilations: int32 [2], replicated, may hold values from 1 to 8, as said below
- band_width: int32 [1], replicated, may hold values from 384 to 511
- tile_table: int32 [32, 12], P('pos'), may hold values from 0 to 11, each once within a row
- cotangent: bfloat16 [384, 128, 128], P(('pos', 'diag')), may hold values from -6 to 6
Outputs:
- bin_grads: float32 [12288, 256], P(('pos', 'diag'))
- left_grads: float32 [256, 64], replicated
- right_grads: float32 [256, 64], replicated
- kern_grads: float32 [2, 9, 64, 64], replicated
- out_grad: float32 [64], replicated
Inputs may be any that keep to these rules, and one draw needn't show every extreme that they name: `dilations`: one of the two convolutions has dilation 8. `tile_table`: each row holds every tile number of its range once.
All inputs are finite; a program needn't handle non-finite values.
Results may differ from a plain program's by a relative error of at most 0.028.
Values may be sent and summed in bfloat16 or wider, within the bound.
A program may use at most 64 MiB of HBM per device.

v0:
```python
import jax
import jax.numpy as jnp
from jax import lax
from jax.sharding import PartitionSpec as P

FEAT = 256
CHAN = 64
TILE = 128
DIAGS = 4
DMAX = 8
TILE_ROWS = 3


OFFSETS = ((-1, -1), (-1, 0), (-1, 1), (0, -1), (0, 0), (0, 1), (1, -1), (1, 0), (1, 1))


def from_behind(block, axis, distance):
    devices = range(lax.axis_size(axis))
    route = [(i - distance, i) for i in devices if i - distance in devices]
    return lax.ppermute(block, axis, route)


def silu_slope(values):
    gate = jax.nn.sigmoid(values)
    return gate * (1.0 + values * (1.0 - gate))


def pad_planes(planes):
    return jnp.pad(planes, ((0, 0), (DMAX, DMAX), (DMAX, DMAX)))


def window_at(padded, shape, row_shift, col_shift):
    anchor = jnp.zeros((), jnp.int32)
    return lax.dynamic_slice(padded, (anchor, DMAX + row_shift, DMAX + col_shift), shape)


def conv_forward(planes, kernel, spread):
    padded = pad_planes(planes)
    summed = jnp.zeros((CHAN, TILE * TILE), jnp.float32)
    for tap_index, (row_step, col_step) in enumerate(OFFSETS):
        window = window_at(padded, planes.shape, row_step * spread, col_step * spread)
        summed = summed + jnp.dot(
            kernel[tap_index], window.reshape(CHAN, -1), preferred_element_type=jnp.float32
        )
    return summed.reshape(planes.shape)


def conv_input_grad(slopes, kernel, spread):
    padded = pad_planes(slopes)
    summed = jnp.zeros((CHAN, TILE * TILE), jnp.float32)
    for tap_index, (row_step, col_step) in enumerate(OFFSETS):
        window = window_at(padded, slopes.shape, -row_step * spread, -col_step * spread)
        summed = summed + lax.dot_general(
            kernel[tap_index],
            window.reshape(CHAN, -1),
            (((0,), (0,)), ((), ())),
            preferred_element_type=jnp.float32,
        )
    return summed.reshape(slopes.shape)


def conv_kernel_grad(slopes, planes, spread):
    padded = pad_planes(planes)
    flat_slopes = slopes.reshape(CHAN, -1)
    pieces = []
    for tap_index, (row_step, col_step) in enumerate(OFFSETS):
        window = window_at(padded, planes.shape, row_step * spread, col_step * spread)
        pieces.append(
            lax.dot_general(
                flat_slopes,
                window.reshape(CHAN, -1),
                (((1,), (1,)), ((), ())),
                preferred_element_type=jnp.float32,
            )
        )
    return jnp.stack(pieces)


def add_rows(target, update, row_start):
    current = lax.dynamic_slice_in_dim(target, row_start, update.shape[0], 0)
    return lax.dynamic_update_slice_in_dim(target, current + update, row_start, 0)


def shards(
    bin_features,
    left_weight,
    right_weight,
    kernel_one,
    kernel_two,
    out_weight,
    dilations,
    band_width,
    tile_table,
    cotangent,
):
    highest = lax.Precision.HIGHEST
    pos_index = lax.axis_index("pos")
    diag_index = lax.axis_index("diag")
    group_bins = TILE_ROWS * TILE
    halo_bins = (DIAGS - 1) * TILE
    total_bins = group_bins * lax.axis_size("pos")
    slot_count = cotangent.shape[0]
    left_wide = left_weight.astype(jnp.float32)
    right_wide = right_weight.astype(jnp.float32)
    gathered = lax.all_gather(bin_features, "diag", axis=0, tiled=True)
    next_part = from_behind(gathered, "pos", -1)
    extended = jnp.concatenate([gathered, next_part], 0)
    tile_ids = lax.dynamic_slice_in_dim(tile_table[0], diag_index * slot_count, slot_count, 0)
    first_bin = pos_index * group_bins
    offsets_in = jnp.arange(TILE, dtype=jnp.int32)
    band_limit = band_width[0]
    out_wide = out_weight.astype(jnp.float32)

    def slot_step(carry, inputs):
        ext_grads, left_acc, right_acc, kern_acc, out_acc = carry
        tile_id, cot_tile = inputs
        upper_row = tile_id // DIAGS
        lower_row = upper_row + tile_id % DIAGS
        upper_rows = lax.dynamic_slice_in_dim(extended, upper_row * TILE, TILE, 0)
        lower_rows = lax.dynamic_slice_in_dim(extended, lower_row * TILE, TILE, 0)
        left_proj = jnp.dot(upper_rows, left_weight, preferred_element_type=jnp.float32).astype(
            jnp.bfloat16
        )
        right_proj = jnp.dot(lower_rows, right_weight, preferred_element_type=jnp.float32).astype(
            jnp.bfloat16
        )
        pair_init = (
            left_proj.astype(jnp.float32).T[:, :, None]
            + right_proj.astype(jnp.float32).T[:, None, :]
        ).astype(jnp.bfloat16)
        first_pre = conv_forward(pair_init, kernel_one, dilations[0])
        first_map = jax.nn.silu(first_pre).astype(jnp.bfloat16)
        second_pre = conv_forward(first_map, kernel_two, dilations[1])
        second_map = jax.nn.silu(second_pre).astype(jnp.bfloat16)
        upper_bin = first_bin + upper_row * TILE + offsets_in[:, None]
        lower_bin = first_bin + lower_row * TILE + offsets_in[None, :]
        in_band = (
            (lower_bin >= upper_bin)
            & (lower_bin - upper_bin <= band_limit)
            & (lower_bin < total_bins)
        )
        masked = jnp.where(in_band, cot_tile, jnp.zeros_like(cot_tile))
        out_acc = out_acc + jnp.dot(
            second_map.reshape(CHAN, -1), masked.reshape(-1), preferred_element_type=jnp.float32
        )
        slope_two = (
            out_wide[:, None, None] * masked.astype(jnp.float32)[None] * silu_slope(second_pre)
        ).astype(jnp.bfloat16)
        kern_two = conv_kernel_grad(slope_two, first_map, dilations[1])
        back_one = conv_input_grad(slope_two, kernel_two, dilations[1])
        slope_one = (back_one * silu_slope(first_pre)).astype(jnp.bfloat16)
        kern_one = conv_kernel_grad(slope_one, pair_init, dilations[0])
        back_init = conv_input_grad(slope_one, kernel_one, dilations[0])
        left_grad = jnp.sum(back_init, 2).T
        right_grad = jnp.sum(back_init, 1).T
        upper_term = jnp.dot(left_grad, left_wide.T, precision=highest)
        lower_term = jnp.dot(right_grad, right_wide.T, precision=highest)
        left_acc = left_acc + jnp.dot(
            upper_rows.astype(jnp.float32).T, left_grad, precision=highest
        )
        right_acc = right_acc + jnp.dot(
            lower_rows.astype(jnp.float32).T, right_grad, precision=highest
        )
        ext_grads = add_rows(ext_grads, upper_term, upper_row * TILE)
        ext_grads = add_rows(ext_grads, lower_term, lower_row * TILE)
        kern_acc = kern_acc + jnp.stack([kern_one, kern_two])
        return ((ext_grads, left_acc, right_acc, kern_acc, out_acc), None)

    start = (
        jnp.zeros(extended.shape, jnp.float32),
        jnp.zeros((FEAT, CHAN), jnp.float32),
        jnp.zeros((FEAT, CHAN), jnp.float32),
        jnp.zeros((2, 9, CHAN, CHAN), jnp.float32),
        jnp.zeros((CHAN,), jnp.float32),
    )
    (ext_grads, left_acc, right_acc, kern_acc, out_acc), unused = lax.scan(
        slot_step, start, (tile_ids, cotangent)
    )
    arrived = from_behind(ext_grads[group_bins:].astype(jnp.bfloat16), "pos", 1).astype(jnp.float32)
    group_part = jnp.concatenate(
        [ext_grads[:halo_bins] + arrived, ext_grads[halo_bins:group_bins]], 0
    )
    owned_grads = lax.psum_scatter(
        group_part.astype(jnp.bfloat16), "diag", scatter_dimension=0, tiled=True
    ).astype(jnp.float32)
    kern_sum, left_sum, right_sum, out_sum = lax.psum(
        (kern_acc, left_acc, right_acc, out_acc), ("pos", "diag")
    )
    range_count = lax.axis_size("pos")
    return (
        owned_grads,
        left_sum / range_count,
        right_sum / range_count,
        kern_sum / range_count,
        out_sum / range_count,
    )


def solution(mesh):
    placed = (
        P(("pos", "diag"), None),
        P(),
        P(),
        P(),
        P(),
        P(),
        P(),
        P(),
        P("pos", None),
        P(("pos", "diag"), None, None),
    )
    return jax.shard_map(
        shards,
        mesh=mesh,
        in_specs=placed,
        out_specs=(P(("pos", "diag"), None), P(), P(), P(), P()),
        check_vma=False,
    )
```

profile of v0, /device:TPU:1, one launch (start us, length us, event | category | flops | bytes accessed | tf_op | source)
XLA Modules:
  0.0 633.3 jit_solution(9412662457151374874)
XLA Ops:
  8.1 10.9 %all_gather.3 = bf16[384,256]{1,0:T(8,128)(2,1)S(1)} all-gather(bf16[96,256]{1,0:T(8,128)(2,1)} %param.12), channel_id=1, replica_groups=mesh['pos'=32,'diag'=4] {'diag'}, dimensions={0}, use_global_device_ids=true | all-gather | bytes 245760 | tf_op jit(solution)/shard_map/all_gather | solution.py:105
  19.0 5.3 collective-permute-start
  34.4 368.9 %while.23 = (s32[]{:T(128)}, f32[768,256]{1,0:T(8,128)}, f32[256,64]{0,1:T(8,128)}, f32[256,64]{0,1:T(8,128)}, f32[2,9,64,64]{3,2,1,0:T(8,128)}, /*index=5*/f32[...) while((s32[]{:T(128)}, f32[768,256]{1,0:T(8,128)}, ...), condition=%wide.region_3.4_spmd.clone.clone, body=%wide.region_0.3_spmd.clone.clone.sunk | while | flops 7456907776 | bytes 641309184 | solution.py:176
  39.6 2.2 fusion.619
  43.5 10.1 %fusion.623 = (bf16[128,8,8,128]{3,2,1,0:T(8,128)(2,1)S(1)}, bf16[128,8,8,128]{3,2,1,0:T(8,128)(2,1)S(1)}, bf16[128,8,8,128]{3,2,1,0:T(8,128)(2,1)S(1)}, bf16[12...) fusion(s32[]{:T(128)} %get-tuple-element.902, ...), kind=kLoop, calls=%fused_computation.213.clone.1 | loop fusion | bytes 18874376 | tf_op jit(solution)/shard_map/while
  61.7 11.3 %fusion.626 = (bf16[128,8,8,128]{3,2,1,0:T(8,128)(2,1)S(1)}, bf16[128,8,8,128]{3,2,1,0:T(8,128)(2,1)S(1)}, bf16[128,8,8,128]{3,2,1,0:T(8,128)(2,1)S(1)}, bf16[12...) fusion(s32[]{:T(128)} %get-tuple-element.905, ...), kind=kLoop, calls=%fused_computation.225.clone.1 | loop fusion | bytes 18874376 | tf_op jit(solution)/shard_map/while
  73.0 2.3 fusion.627
  83.5 2.5 fusion.631
  97.1 10.4 %fusion.629 = (bf16[128,8,8,128]{3,2,1,0:T(8,128)(2,1)S(1)}, bf16[128,8,8,128]{3,2,1,0:T(8,128)(2,1)}, bf16[128,8,8,128]{3,2,1,0:T(8,128)(2,1)S(1)}, bf16[128,8,...) fusion(s32[]{:T(128)} %get-tuple-element.903, ...), kind=kLoop, calls=%fused_computation.118.clone.1 | loop fusion | bytes 18874376 | tf_op jit(solution)/shard_map/while
  128.2 10.8 %fusion.633 = (bf16[128,8,8,128]{3,2,1,0:T(8,128)(2,1)S(1)}, bf16[128,8,8,128]{3,2,1,0:T(8,128)(2,1)}, bf16[128,8,8,128]{3,2,1,0:T(8,128)(2,1)}, bf16[128,8,8,12...) fusion(s32[]{:T(128)} %get-tuple-element.900, ...), kind=kLoop, calls=%fused_computation.126.clone.1 | loop fusion | bytes 18874376 | tf_op jit(solution)/shard_map/while
  144.7 2.1 convolution_add_fusion.96
  161.5 2.2 fusion.619
  165.3 10.1 %fusion.623 = (bf16[128,8,8,128]{3,2,1,0:T(8,128)(2,1)S(1)}, bf16[128,8,8,128]{3,2,1,0:T(8,128)(2,1)S(1)}, bf16[128,8,8,128]{3,2,1,0:T(8,128)(2,1)S(1)}, bf16[12...) fusion(s32[]{:T(128)} %get-tuple-element.902, ...), kind=kLoop, calls=%fused_computation.213.clone.1 | loop fusion | bytes 18874376 | tf_op jit(solution)/shard_map/while
  183.5 11.2 %fusion.626 = (bf16[128,8,8,128]{3,2,1,0:T(8,128)(2,1)S(1)}, bf16[128,8,8,128]{3,2,1,0:T(8,128)(2,1)S(1)}, bf16[128,8,8,128]{3,2,1,0:T(8,128)(2,1)S(1)}, bf16[12...) fusion(s32[]{:T(128)} %get-tuple-element.905, ...), kind=kLoop, calls=%fused_computation.225.clone.1 | loop fusion | bytes 18874376 | tf_op jit(solution)/shard_map/while
  194.8 2.3 fusion.627
  205.3 2.3 fusion.631
  218.6 10.4 %fusion.629 = (bf16[128,8,8,128]{3,2,1,0:T(8,128)(2,1)S(1)}, bf16[128,8,8,128]{3,2,1,0:T(8,128)(2,1)}, bf16[128,8,8,128]{3,2,1,0:T(8,128)(2,1)S(1)}, bf16[128,8,...) fusion(s32[]{:T(128)} %get-tuple-element.903, ...), kind=kLoop, calls=%fused_computation.118.clone.1 | loop fusion | bytes 18874376 | tf_op jit(solution)/shard_map/while
  250.9 10.8 %fusion.633 = (bf16[128,8,8,128]{3,2,1,0:T(8,128)(2,1)S(1)}, bf16[128,8,8,128]{3,2,1,0:T(8,128)(2,1)}, bf16[128,8,8,128]{3,2,1,0:T(8,128)(2,1)}, bf16[128,8,8,12...) fusion(s32[]{:T(128)} %get-tuple-element.900, ...), kind=kLoop, calls=%fused_computation.126.clone.1 | loop fusion | bytes 18874376 | tf_op jit(solution)/shard_map/while
  267.3 2.1 convolution_add_fusion.96
  284.1 2.2 fusion.619
  287.9 10.1 %fusion.623 = (bf16[128,8,8,128]{3,2,1,0:T(8,128)(2,1)S(1)}, bf16[128,8,8,128]{3,2,1,0:T(8,128)(2,1)S(1)}, bf16[128,8,8,128]{3,2,1,0:T(8,128)(2,1)S(1)}, bf16[12...) fusion(s32[]{:T(128)} %get-tuple-element.902, ...), kind=kLoop, calls=%fused_computation.213.clone.1 | loop fusion | bytes 18874376 | tf_op jit(solution)/shard_map/while
  306.2 11.2 %fusion.626 = (bf16[128,8,8,128]{3,2,1,0:T(8,128)(2,1)S(1)}, bf16[128,8,8,128]{3,2,1,0:T(8,128)(2,1)S(1)}, bf16[128,8,8,128]{3,2,1,0:T(8,128)(2,1)S(1)}, bf16[12...) fusion(s32[]{:T(128)} %get-tuple-element.905, ...), kind=kLoop, calls=%fused_computation.225.clone.1 | loop fusion | bytes 18874376 | tf_op jit(solution)/shard_map/while
  317.4 2.3 fusion.627
  327.9 2.3 fusion.631
  341.3 10.4 %fusion.629 = (bf16[128,8,8,128]{3,2,1,0:T(8,128)(2,1)S(1)}, bf16[128,8,8,128]{3,2,1,0:T(8,128)(2,1)}, bf16[128,8,8,128]{3,2,1,0:T(8,128)(2,1)S(1)}, bf16[128,8,...) fusion(s32[]{:T(128)} %get-tuple-element.903, ...), kind=kLoop, calls=%fused_computation.118.clone.1 | loop fusion | bytes 18874376 | tf_op jit(solution)/shard_map/while
  371.5 2.0 maximum_add_fusion.2
  373.5 10.8 %fusion.633 = (bf16[128,8,8,128]{3,2,1,0:T(8,128)(2,1)S(1)}, bf16[128,8,8,128]{3,2,1,0:T(8,128)(2,1)}, bf16[128,8,8,128]{3,2,1,0:T(8,128)(2,1)}, bf16[128,8,8,12...) fusion(s32[]{:T(128)} %get-tuple-element.900, ...), kind=kLoop, calls=%fused_computation.126.clone.1 | loop fusion | bytes 18874376 | tf_op jit(solution)/shard_map/while
  389.9 2.1 convolution_add_fusion.96
  403.3 67.4 %psum.31 = f32[64]{0:T(128)S(1)} all-reduce(f32[64]{0:T(128)} %get-tuple-element.391), channel_id=1, replica_groups=mesh['pos'=32,'diag'=4] {'pos','diag'}, use_global_device_ids=true, to_apply=%region_8.9 | all-reduce | flops 64 | bytes 512 | tf_op jit(solution)/shard_map/psum | solution.py:186
  471.7 2.0 collective-permute-start.1
  474.4 2.0 collective-permute-done.1
  478.1 142.6 %all-reduce.7.cloned.1.call-done = (f32[256,64]{0,1:T(8,128)}, f32[256,64]{0,1:T(8,128)}, f32[2,9,64,64]{3,2,1,0:T(8,128)}) async-done(((f32[256,64]{0,1:T(8,128)}, f32[256,64]{0,1:T(8,128)}, f32[2,9,64,64]{3,2,1,0:T(8,128)}), (f32[256,64]{0,1:T(8,128)}, f32[256,64]{0,1:T(8,128)}, f32[2,9,64,64]{3,2,1,0:T(8,128)})) %all-reduce.7.cloned.1.call-update) | async-done | bytes 426000 | tf_op jit(solution)/shard_map/psum | solution.py:186
  (418 shorter events, 213.9 us)
Async XLA Ops:
  8.0 25.3 %copy-start = (s32[1,12]{1,0:T(1,128)S(1)}, s32[1,12]{1,0:T(1,128)}, u32[]{:S(2)}) copy-start(s32[1,12]{1,0:T(1,128)} %param.20) | copy-start | bytes 148
  8.0 612.7 %all-reduce.7.cloned.1.call-start = ((), (), s32[]{:S(2)}) async-start(), calls=%async_computation.2 | async-start | bytes 1441792 | tf_op jit(solution)/shard_map/psum | solution.py:186
  19.0 14.4 %collective-permute-start = (bf16[384,256]{1,0:T(8,128)(2,1)S(1)}, bf16[384,256]{1,0:T(8,128)(2,1)S(1)}, u32[]{:S(2)}, u32[]{:S(2)}) collective-permute-start(bf16[384,256]{1,0:T(8,128)(2,1)S(1)} %all_gather.3), channel_id=1, source_target_pairs={{4,0},{8,4},{12,8},{16,12},{20,16},{24,20},{28,24},{32,28},{36,32}... | collective-permute-start | bytes 589832 | tf_op jit(solution)/shard_map/ppermute | solution.py:20
  34.4 9.1 %copy-start.13 = (bf16[768,256]{1,0:T(8,128)(2,1)}, bf16[768,256]{1,0:T(8,128)(2,1)S(1)}, u32[]{:S(2)}) copy-start(bf16[768,256]{1,0:T(8,128)(2,1)S(1)} %get-tuple-element.897) | copy-start | bytes 1179652 | tf_op jit(solution)/shard_map/while
  34.4 9.1 %copy-start.28 = (s32[3]{0:T(128)}, s32[3]{0:T(128)S(1)}, u32[]{:S(2)}) copy-start(s32[3]{0:T(128)S(1)} %get-tuple-element.892) | copy-start | bytes 40 | tf_op jit(solution)/shard_map/while
  39.6 3.8 copy-start.19
  43.5 10.1 %copy-start.7 = (bf16[64,128,128]{2,0,1:T(8,128)(2,1)}, bf16[64,128,128]{2,0,1:T(8,128)(2,1)S(1)}, u32[]{:S(2)}) copy-start(bf16[64,128,128]{2,0,1:T(8,128)(2,1)S(1)} %get-tuple-element.786) | copy-start | bytes 6291460 | tf_op jit(solution)/shard_map/while
  83.5 2.5 copy-start.27
  83.5 2.5 copy-start.30
  150.6 3.5 copy-start.22
  150.6 5.4 copy-start.29
  152.0 4.0 copy-start.26
  152.2 3.8 copy-start.24
  156.2 9.1 %copy-start.13 = (bf16[768,256]{1,0:T(8,128)(2,1)}, bf16[768,256]{1,0:T(8,128)(2,1)S(1)}, u32[]{:S(2)}) copy-start(bf16[768,256]{1,0:T(8,128)(2,1)S(1)} %get-tuple-element.897) | copy-start | bytes 1179652 | tf_op jit(solution)/shard_map/while
  156.2 9.1 %copy-start.28 = (s32[3]{0:T(128)}, s32[3]{0:T(128)S(1)}, u32[]{:S(2)}) copy-start(s32[3]{0:T(128)S(1)} %get-tuple-element.892) | copy-start | bytes 40 | tf_op jit(solution)/shard_map/while
  161.4 3.8 copy-start.19
  165.3 10.1 %copy-start.7 = (bf16[64,128,128]{2,0,1:T(8,128)(2,1)}, bf16[64,128,128]{2,0,1:T(8,128)(2,1)S(1)}, u32[]{:S(2)}) copy-start(bf16[64,128,128]{2,0,1:T(8,128)(2,1)S(1)} %get-tuple-element.786) | copy-start | bytes 6291460 | tf_op jit(solution)/shard_map/while
  273.2 3.6 copy-start.22
  273.2 5.4 copy-start.29
  274.6 4.0 copy-start.26
  274.9 3.8 copy-start.24
  278.8 9.1 %copy-start.13 = (bf16[768,256]{1,0:T(8,128)(2,1)}, bf16[768,256]{1,0:T(8,128)(2,1)S(1)}, u32[]{:S(2)}) copy-start(bf16[768,256]{1,0:T(8,128)(2,1)S(1)} %get-tuple-element.897) | copy-start | bytes 1179652 | tf_op jit(solution)/shard_map/while
  278.9 9.1 %copy-start.28 = (s32[3]{0:T(128)}, s32[3]{0:T(128)S(1)}, u32[]{:S(2)}) copy-start(s32[3]{0:T(128)S(1)} %get-tuple-element.892) | copy-start | bytes 40 | tf_op jit(solution)/shard_map/while
  284.1 3.8 copy-start.19
  287.9 10.1 %copy-start.7 = (bf16[64,128,128]{2,0,1:T(8,128)(2,1)}, bf16[64,128,128]{2,0,1:T(8,128)(2,1)S(1)}, u32[]{:S(2)}) copy-start(bf16[64,128,128]{2,0,1:T(8,128)(2,1)S(1)} %get-tuple-element.786) | copy-start | bytes 6291460 | tf_op jit(solution)/shard_map/while
  395.8 3.6 copy-start.22
  395.9 5.4 copy-start.29
  397.3 4.0 copy-start.26
  397.5 3.8 copy-start.24
  403.3 222.3 %copy-start.1 = (s32[1,12]{1,0:T(1,128)S(1)}, s32[1,12]{1,0:T(1,128)}, u32[]{:S(2)}) copy-start(s32[1,12]{1,0:T(1,128)} %param.20) | copy-start | bytes 148
  471.7 4.6 collective-permute-start.1
  473.8 150.3 %reduce-scatter.2.cloned.1.call-start = ((), (), s32[]{:S(2)}) async-start(), calls=%async_computation.1 | async-start | bytes 245760 | tf_op jit(solution)/shard_map/reduce_scatter | solution.py:183
  (64 other events, 96.5 us)
Sparse Core Ops, SparseCore 0:
  473.9 146.7 all-reduce.6
Sparse Core Ops, SparseCore 1:
  478.2 19.3 reduce-scatter.1
where the time goes:
time: 637 us; the launch traced here: 633 us
  matrix products  173 us (27%)
  local copies, waits for them, and re-layouts  148 us (23%)
  waiting for transfers between devices  145 us (23%)
  blocking collectives  78.3 us (12%)
  other arithmetic  49.6 us (8%)
  between operations  19.7 us (3%)
  loops' own time  12.9 us (2%)
  starting transfers between devices  7.44 us (1%)
    psum x1, waiting for transfers between devices, shards(): lax.psum((kern_acc, left_acc, right_acc, out_acc), ('pos', 'diag'))  143 us
    while x195, local copies, waits for them, and re-layouts  140 us
    psum x1, blocking collectives, shards(): lax.psum((kern_acc, left_acc, right_acc, out_acc), ('pos', 'diag'))  67.4 us
    dot_general x54, matrix products, conv_kernel_grad(): lax.dot_general(flat_slopes, window.reshape(CHAN, -1), (((1,), (1,)), (()...  56.6 us
    dot_general x54, matrix products, conv_input_grad(): lax.dot_general(kernel[tap_index], window.reshape(CHAN, -1), (((0,), (0,)...  49.9 us
    dot_general x54, matrix products, conv_forward(): jnp.dot(kernel[tap_index], window.reshape(CHAN, -1), preferred_element_ty...  46.9 us
    another operation x1, loops' own time, shards(): lax.scan(slot_step, start, (tile_ids, cotangent))  12.9 us
  transfers between devices with their start and end apart: 4, of which 2 were waited for; matrix products, arithmetic and copies ran while one was open for 2% of the time, Pallas kernels for 0%

commit v1 on v0

v1 whole, which is shorter than its diff:
```python
import jax
import jax.numpy as jnp
from jax import lax
from jax.experimental import pallas as pl
from jax.experimental.pallas import tpu as pltpu
from jax.sharding import PartitionSpec as P

TILE = 128
CHAN = 64
BF = jnp.bfloat16
F32 = jnp.float32
NT = (((1,), (1,)), ((), ()))
ROWS = 8
BLOCKS = TILE // ROWS
STRIDE = TILE + 2 * ROWS
MESH = pl.DeviceIdType.MESH
NEAR = 8
FAR = 16
PIECE = 8
SHARE = FAR * PIECE
PAYLOAD = NEAR * SHARE


def mm(a, b):
    return jnp.dot(a, b, preferred_element_type=F32)


def mm_nt(a, b):
    return lax.dot_general(a, b, NT, preferred_element_type=F32)


def tile_kernel(
    dil, bandw, table, feats, wl, wr, k1, k2, outw, cot,
    rows_out, pay_out,
    rows_acc, lr_acc, wmat, hp, d1, s2p, msk, bvar, gat, rsacc, edge, csacc, gacc, k1a, k1b, ogacc, rsm, lsh, rsh, idxr,
):
    e1 = dil[0]
    e2 = dil[1]
    band = bandw[0]
    group_bins = feats.shape[0] // 2
    first_bin = lax.axis_index("pos") * group_bins
    total_bins = lax.axis_size("pos") * group_bins
    first_slot = lax.axis_index("diag") * cot.shape[0]
    n_tiles = cot.shape[0]
    lane = lax.broadcasted_iota(jnp.int32, (CHAN, TILE), 1)

    for which, ref in ((0, k1), (1, k2)):
        wide = ref[...].astype(F32)
        w_rows = []
        v_rows = []
        for p in range(3):
            w_rows.append(jnp.concatenate([wide[3 * q + p] for q in range(3)], axis=1))
            v_rows.append(jnp.concatenate([wide[3 * p + q] for q in range(3)], axis=1))
        w = jnp.concatenate(w_rows, axis=0)
        v = jnp.concatenate(v_rows, axis=0)
        if which == 0:
            wmat[0] = (w * 0.5).astype(BF)
            wmat[1] = (v * 0.5).astype(BF)
            wmat[2] = w.T.astype(BF)
            wmat[3] = v.T.astype(BF)
        else:
            wmat[4] = (w * 0.5).astype(BF)
            wmat[5] = (v.T * 0.5).astype(BF)

    rows_acc[...] = jnp.zeros_like(rows_acc)
    lr_acc[...] = jnp.zeros_like(lr_acc)
    gacc[...] = jnp.zeros_like(gacc)
    k1a[...] = jnp.zeros_like(k1a)
    k1b[...] = jnp.zeros_like(k1b)
    ogacc[...] = jnp.zeros_like(ogacc)
    zero_rows = jnp.zeros((ROWS, CHAN, TILE), BF)
    for ref in (hp, s2p):
        ref[0:ROWS] = zero_rows
        ref[ROWS + TILE:] = zero_rows
    yy = lax.broadcasted_iota(jnp.int32, (TILE, TILE), 0)
    nn = lax.broadcasted_iota(jnp.int32, (TILE, TILE), 1)
    shifted = yy + (nn // 32 - 1) * e1
    rsm[...] = jnp.where((shifted >= 0) & (shifted < TILE) & (nn < 96), 1.0, 0.0).astype(BF)
    idxr[...] = jnp.where(lane < e1, 32, jnp.where(lane >= TILE - e1, 64, 0))
    outh = jnp.broadcast_to(outw[...].astype(F32), (TILE, CHAN)).T * 0.5
    lane_mod = lane % 32

    def shift_lanes(v, distance):
        width = v.shape[-1]
        ln = lax.broadcasted_iota(jnp.int32, v.shape, 1)
        rolled = pltpu.roll(v, lax.rem(width - distance, width), 1)
        src = ln + distance
        return jnp.where((src >= 0) & (src < TILE), rolled, 0.0)

    def stack3(v, step):
        return jnp.concatenate(
            [shift_lanes(v, -step), v, shift_lanes(v, step)], axis=0
        )

    for t in range(n_tiles):
        tid = table[0, first_slot + t]
        upper = lax.div(tid, 4)
        lower = upper + lax.rem(tid, 4)
        upper_at = pl.multiple_of(upper * TILE, TILE)
        lower_at = pl.multiple_of(lower * TILE, TILE)
        f_up = feats[pl.ds(upper_at, TILE), :]
        f_lo = feats[pl.ds(lower_at, TILE), :]
        left = mm_nt(wl[...], f_up).astype(BF).astype(F32)
        right = mm_nt(wr[...], f_lo).astype(BF).astype(F32)
        left3 = stack3(left, e1).astype(BF)
        right3 = stack3(right, e1).astype(BF)
        lsh[...] = left3
        rsh[...] = right3
        a_out = mm(wmat[0], left3)
        b_out = mm(wmat[1], right3)
        am, a0, ap = a_out[0:64], a_out[64:128], a_out[128:192]
        bm, b0, bp = b_out[0:64], b_out[64:128], b_out[128:192]
        bvar[0] = bm + b0 + bp
        bvar[1] = b0 + bp
        bvar[2] = bm + b0
        variants = (am + a0 + ap, a0 + ap, am + a0)
        for k in range(4):
            gat[k] = jnp.concatenate(
                [va[:, 32 * k:32 * k + 32] for va in variants] + [jnp.zeros((CHAN, 32), F32)], axis=1
            )
        xx = lax.broadcasted_iota(jnp.int32, (TILE, TILE), 0)
        y2 = lax.broadcasted_iota(jnp.int32, (TILE, TILE), 1)
        gap = (lower - upper) * TILE + y2 - xx
        inside = (gap >= 0) & (gap <= band) & (first_bin + lower * TILE + y2 < total_bins)
        msk[...] = jnp.where(inside, cot[t].astype(F32), 0.0)
        csacc[...] = jnp.zeros_like(csacc)

        def phase_one(i, carry):
            values = gat[lax.div(i, 4)]
            base = idxr[...] + lax.rem(i, 4) * ROWS
            for j in range(ROWS):
                x = i * ROWS + j
                kind = jnp.where(x < e1, 1, jnp.where(x >= TILE - e1, 2, 0))
                u = jnp.take_along_axis(values, base + j, axis=1) + bvar[kind]
                th = jnp.tanh(u)
                w = u * th
                hp[x + ROWS] = (u + w).astype(BF)
                d1[x] = ((1.0 + th) * ((1.0 + u) - w)).astype(BF)
            return carry

        lax.fori_loop(0, BLOCKS, phase_one, 0)

        def taps(ref, x, spread):
            return jnp.concatenate(
                [ref[x + ROWS - spread], ref[x + ROWS], ref[x + ROWS + spread]], axis=0
            )

        def phase_two(i, carry):
            lefts = []
            rights = []
            og = ogacc[...]
            for p in range(ROWS // 2):
                x = i * ROWS + 2 * p
                rhs = jnp.concatenate([taps(hp, x, e2), taps(hp, x + 1, e2)], axis=1)
                z = mm(wmat[4], rhs)
                parts = []
                for j in range(2):
                    cols = z[:, j * TILE:(j + 1) * TILE]
                    u = (
                        cols[64:128]
                        + shift_lanes(cols[0:64], -e2)
                        + shift_lanes(cols[128:192], e2)
                    )
                    th = jnp.tanh(u)
                    w = u * th
                    m = msk[pl.ds(x + j, 1), :]
                    og = og + (u + w) * m
                    s = (outh * m) * ((1.0 + th) * ((1.0 + u) - w))
                    s16 = s.astype(BF)
                    s2p[x + j + ROWS] = s16
                    parts.append(jnp.concatenate(
                        [shift_lanes(s, e2).astype(BF), s16, shift_lanes(s, -e2).astype(BF)], axis=0
                    ))
                lefts.append(jnp.concatenate(parts, axis=1))
                rights.append(rhs)
            ogacc[...] = og
            gacc[...] += mm_nt(jnp.concatenate(lefts, axis=1), jnp.concatenate(rights, axis=1))
            return carry

        lax.fori_loop(0, BLOCKS, phase_two, 0)

        def phase_three(i, carry):
            total = jnp.zeros((CHAN, TILE), F32)
            slot = jnp.where(i == 0, 0, jnp.where(i == BLOCKS - 1, 1, 2))
            acc = rsacc[lax.div(i, 4)]
            for p in range(ROWS // 2):
                x = i * ROWS + 2 * p
                rhs = jnp.concatenate([taps(s2p, x, -e2), taps(s2p, x + 1, -e2)], axis=1)
                z = mm(wmat[5], rhs)
                for j in range(2):
                    cols = z[:, j * TILE:(j + 1) * TILE]
                    back = (
                        cols[64:128]
                        + shift_lanes(cols[0:64], e2)
                        + shift_lanes(cols[128:192], -e2)
                    )
                    s = back * d1[x + j].astype(F32)
                    s16 = s.astype(BF)
                    total = total + s
                    edge[slot, 2 * p + j] = s16
                    sums = mm(s16, rsm[...])
                    acc = jnp.where(lane_mod == lax.rem(x + j, 32), sums, acc)
            rsacc[lax.div(i, 4)] = acc
            csacc[...] += total
            return carry

        lax.fori_loop(0, BLOCKS, phase_three, 0)

        rs = jnp.concatenate(
            [
                jnp.concatenate([rsacc[k][:, 32 * b:32 * b + 32] for k in range(4)], axis=1)
                for b in range(3)
            ],
            axis=0,
        )
        cs0 = csacc[...]
        head = jnp.zeros((CHAN, TILE), F32)
        tail = jnp.zeros((CHAN, TILE), F32)
        for j in range(ROWS):
            head = head + jnp.where(j < e1, edge[0, j].astype(F32), 0.0)
            tail = tail + jnp.where(j >= ROWS - e1, edge[1, j].astype(F32), 0.0)
        cs = jnp.concatenate([cs0 - head, cs0, cs0 - tail], axis=0)
        rs16 = rs.astype(BF)
        cs16 = cs.astype(BF)
        k1a[...] += mm_nt(rs16, lsh[...])
        k1b[...] += mm_nt(cs16, rsh[...])
        yl = mm(wmat[2], rs16)
        yr = mm(wmat[3], cs16)
        lg = yl[64:128] + shift_lanes(yl[0:64], e1) + shift_lanes(yl[128:192], -e1)
        rg = yr[64:128] + shift_lanes(yr[0:64], e1) + shift_lanes(yr[128:192], -e1)
        lr_acc[0:64] += mm(lg.astype(BF), f_up)
        lr_acc[64:128] += mm(rg.astype(BF), f_lo)
        both = jnp.concatenate([lg, rg], axis=0).T
        left_half = lax.broadcasted_iota(jnp.int32, (TILE, TILE), 1) < CHAN
        rows_acc[pl.ds(upper_at, TILE), :] += jnp.where(left_half, both, 0.0)
        rows_acc[pl.ds(lower_at, TILE), :] += jnp.where(left_half, 0.0, both)

    for a in range(3):
        for b in range(3):
            tap = 3 * a + b
            one = (
                k1a[64 * b:64 * b + 64, 64 * a:64 * a + 64]
                + k1b[64 * a:64 * a + 64, 64 * b:64 * b + 64]
            )
            two = gacc[64 * b:64 * b + 64, 64 * a:64 * a + 64]
            pay_out[64 * tap:64 * tap + 64] = jnp.concatenate([one, two], axis=1).astype(BF)
    pay_out[576:704] = lr_acc[:, 0:TILE].astype(BF)
    pay_out[704:832] = lr_acc[:, TILE:2 * TILE].astype(BF)
    out_row = jnp.sum(ogacc[...].T, axis=0, keepdims=True)
    out_row = jnp.concatenate([out_row, jnp.zeros((1, CHAN), F32)], axis=1)
    pay_out[832:848] = jnp.broadcast_to(out_row, (16, TILE)).astype(BF)
    pay_out[848:] = jnp.zeros((PAYLOAD - 848, TILE), BF)
    rows_out[...] = rows_acc[...].astype(BF)


def tile_call(dilations, band_width, tile_table, feats, wl, wr, k1, k2, outw, cot):
    vm = pl.BlockSpec(memory_space=pltpu.VMEM)
    sm = pl.BlockSpec(memory_space=pltpu.SMEM)
    return pl.pallas_call(
        tile_kernel,
        out_shape=(
            jax.ShapeDtypeStruct((feats.shape[0], 2 * CHAN), BF),
            jax.ShapeDtypeStruct((PAYLOAD, TILE), BF),
        ),
        in_specs=[sm] * 3 + [vm] * 7,
        out_specs=(vm, vm),
        scratch_shapes=[
            pltpu.VMEM((feats.shape[0], 2 * CHAN), F32),
            pltpu.VMEM((2 * CHAN, feats.shape[1]), F32),
            pltpu.VMEM((6, 192, 192), BF),
            pltpu.VMEM((STRIDE, CHAN, TILE), BF),
            pltpu.VMEM((TILE, CHAN, TILE), BF),
            pltpu.VMEM((STRIDE, CHAN, TILE), BF),
            pltpu.VMEM((TILE, TILE), F32),
            pltpu.VMEM((3, CHAN, TILE), F32),
            pltpu.VMEM((4, CHAN, TILE), F32),
            pltpu.VMEM((4, CHAN, TILE), F32),
            pltpu.VMEM((3, ROWS, CHAN, TILE), BF),
            pltpu.VMEM((CHAN, TILE), F32),
            pltpu.VMEM((192, 192), F32),
            pltpu.VMEM((192, 192), F32),
            pltpu.VMEM((192, 192), F32),
            pltpu.VMEM((CHAN, TILE), F32),
            pltpu.VMEM((TILE, TILE), BF),
            pltpu.VMEM((192, TILE), BF),
            pltpu.VMEM((192, TILE), BF),
            pltpu.VMEM((CHAN, TILE), jnp.int32),
        ],
        compiler_params=pltpu.CompilerParams(vmem_limit_bytes=40 * 1024 * 1024),
        name="tile_work",
    )(dilations, band_width, tile_table, feats, wl, wr, k1, k2, outw, cot)


def greet(devices):
    barrier = pltpu.get_barrier_semaphore()
    for device in devices:
        pl.semaphore_signal(barrier, inc=1, device_id=device, device_id_type=MESH)
    pl.semaphore_wait(barrier, len(devices))


def remote(src, dst, send, recv, device):
    return pltpu.make_async_remote_copy(
        src_ref=src, dst_ref=dst, send_sem=send, recv_sem=recv, device_id=device, device_id_type=MESH
    )


def gather_kernel(own_ref, all_ref, send, recv):
    ranges = lax.axis_size("pos")
    members = lax.axis_size("diag")
    pos = lax.axis_index("pos")
    diag = lax.axis_index("diag")
    rows = own_ref.shape[0]
    half = members * rows
    before = (lax.rem(pos + ranges - 1, ranges), diag)
    after = (lax.rem(pos + 1, ranges), diag)
    others = [(pos, lax.rem(diag + k, members)) for k in range(1, members)]
    greet(others + [before, after])

    def place(owner, base):
        return pl.ds(pl.multiple_of(base + owner * rows, 32), rows)

    all_ref[place(diag, 0), :] = own_ref[...]
    copies = []
    first = remote(own_ref, all_ref.at[place(diag, half)], send.at[0], recv.at[0], before)
    first.start()
    for k in range(1, members):
        copy = remote(own_ref, all_ref.at[place(diag, 0)], send.at[k], recv.at[k], others[k - 1])
        copy.start()
        copies.append(copy)
    passed = []
    for k in (1, 3, 2):
        copies[k - 1].wait_recv()
        owner = lax.rem(diag + members - k, members)
        copy = remote(
            all_ref.at[place(owner, 0)],
            all_ref.at[place(owner, half)],
            send.at[members + k - 1],
            recv.at[members + k - 1],
            before,
        )
        copy.start()
        passed.append(copy)
    for copy in copies:
        copy.wait_send()
    first.wait()
    for copy in passed:
        copy.wait()


def gather_call(own):
    vm = pl.BlockSpec(memory_space=pltpu.VMEM)
    members = lax.axis_size("diag")
    return pl.pallas_call(
        gather_kernel,
        out_shape=jax.ShapeDtypeStruct((2 * members * own.shape[0], own.shape[1]), own.dtype),
        in_specs=[vm],
        out_specs=vm,
        scratch_shapes=[
            pltpu.SemaphoreType.DMA((2 * members,)),
            pltpu.SemaphoreType.DMA((2 * members,)),
        ],
        compiler_params=pltpu.CompilerParams(collective_id=0, has_side_effects=True),
        name="gather_bins",
    )(own)


def reduce_kernel(
    rows_ref, pay_ref, wl, wr,
    bin_out, left_out, right_out, kern_out, out_out,
    row_buf, near_buf, near_sum, far_buf, far_all, near_own, all_buf,
    row_send, row_recv, near_send, near_recv, far_send, far_recv,
    back_send, back_recv, last_send, last_recv,
):
    ranges = lax.axis_size("pos")
    members = lax.axis_size("diag")
    pos = lax.axis_index("pos")
    diag = lax.axis_index("diag")
    core = lax.rem(pos, 2)
    chip = lax.div(pos, 2)
    count = bin_out.shape[0]
    half = members * count
    after = lax.rem(pos + 1, ranges)
    before = lax.rem(pos + ranges - 1, ranges)
    across = lax.rem(pos + ranges + 2 * core - 1, ranges)
    near = core * members + diag

    near_ids = [lax.rem(near + k, NEAR) for k in range(1, NEAR)]
    near_devs = [(2 * chip + lax.div(n, members), lax.rem(n, members)) for n in near_ids]
    far_ids = [lax.rem(chip + k, FAR) for k in range(1, FAR)]
    far_devs = [(2 * f + core, diag) for f in far_ids]
    greet(near_devs + far_devs + [(across, d) for d in range(members)])

    def piece(index, size):
        return pl.ds(pl.multiple_of(index * size, size), size)

    near_copies = []
    for k in range(1, NEAR):
        copy = remote(
            pay_ref.at[piece(near_ids[k - 1], SHARE)], near_buf.at[k - 1],
            near_send.at[k - 1], near_recv.at[k - 1], near_devs[k - 1],
        )
        copy.start()
        near_copies.append(copy)
    row_copies = []
    for k in range(1, 2 * members):
        owner = lax.rem(diag + k, members)
        base = 0 if k < members else half
        target = (pos, owner) if k < members else (after, owner)
        copy = remote(
            rows_ref.at[pl.ds(pl.multiple_of(base + owner * count, 32), count)], row_buf.at[k - 1],
            row_send.at[k - 1], row_recv.at[k - 1], target,
        )
        copy.start()
        row_copies.append(copy)

    total = pay_ref[piece(near, SHARE), :].astype(F32)
    for k in range(1, NEAR):
        near_copies[k - 1].wait_recv()
        total = total + near_buf[k - 1].astype(F32)
    near_sum[...] = total
    far_copies = []
    for k in range(1, FAR):
        copy = remote(
            near_sum.at[piece(far_ids[k - 1], PIECE)], far_buf.at[k - 1],
            far_send.at[k - 1], far_recv.at[k - 1], far_devs[k - 1],
        )
        copy.start()
        far_copies.append(copy)

    rows = rows_ref[pl.ds(pl.multiple_of(diag * count, 32), count), :].astype(F32)
    for k in range(1, 2 * members):
        row_copies[k - 1].wait_recv()
        rows = rows + row_buf[k - 1].astype(F32)
    weights = jnp.concatenate([wl[...], wr[...]], axis=0)
    bin_out[...] = mm(rows.astype(BF), weights)

    mine = near_sum[piece(chip, PIECE), :]
    for k in range(1, FAR):
        far_copies[k - 1].wait_recv()
        mine = mine + far_buf[k - 1]
    far_all[piece(chip, PIECE), :] = mine * (1.0 / ranges)
    back_copies = []
    for k in range(1, FAR):
        copy = remote(
            far_all.at[piece(chip, PIECE)], far_all.at[piece(chip, PIECE)],
            back_send.at[k - 1], back_recv.at[k - 1], far_devs[k - 1],
        )
        copy.start()
        back_copies.append(copy)
    for k in range(1, FAR):
        back_copies[k - 1].wait_recv()
    near_own[...] = far_all[...].astype(BF)
    last_copies = []
    for k in range(1, NEAR):
        copy = remote(
            near_own, all_buf.at[piece(near, SHARE)],
            last_send.at[k - 1], last_recv.at[k - 1], near_devs[k - 1],
        )
        copy.start()
        last_copies.append(copy)
    all_buf[piece(near, SHARE), :] = near_own[...]
    for k in range(1, NEAR):
        last_copies[k - 1].wait_recv()

    for tap in range(9):
        block = all_buf[64 * tap:64 * tap + 64, :].astype(F32)
        kern_out[0, tap] = block[:, 0:CHAN]
        kern_out[1, tap] = block[:, CHAN:2 * CHAN]
    for part in range(2):
        block = all_buf[576 + TILE * part:576 + TILE * part + TILE, :].astype(F32)
        left_out[:, TILE * part:TILE * part + TILE] = block[0:CHAN]
        right_out[:, TILE * part:TILE * part + TILE] = block[CHAN:2 * CHAN]
    out_out[...] = all_buf[832:848, :].astype(F32)[0:1, 0:CHAN]

    for copy in near_copies + row_copies + far_copies + back_copies + last_copies:
        copy.wait_send()


def reduce_call(rows, payload, wl, wr):
    vm = pl.BlockSpec(memory_space=pltpu.VMEM)
    members = lax.axis_size("diag")
    count = rows.shape[0] // (2 * members)
    feat = wl.shape[1]
    dma = pltpu.SemaphoreType.DMA
    return pl.pallas_call(
        reduce_kernel,
        out_shape=(
            jax.ShapeDtypeStruct((count, feat), F32),
            jax.ShapeDtypeStruct((CHAN, feat), F32),
            jax.ShapeDtypeStruct((CHAN, feat), F32),
            jax.ShapeDtypeStruct((2, 9, CHAN, CHAN), F32),
            jax.ShapeDtypeStruct((1, CHAN), F32),
        ),
        in_specs=[vm] * 4,
        out_specs=(vm,) * 5,
        scratch_shapes=[
            pltpu.VMEM((2 * members - 1, count, 2 * CHAN), BF),
            pltpu.VMEM((NEAR - 1, SHARE, TILE), BF),
            pltpu.VMEM((SHARE, TILE), F32),
            pltpu.VMEM((FAR - 1, PIECE, TILE), F32),
            pltpu.VMEM((SHARE, TILE), F32),
            pltpu.VMEM((SHARE, TILE), BF),
            pltpu.VMEM((PAYLOAD, TILE), BF),
            dma((2 * members - 1,)), dma((2 * members - 1,)),
            dma((NEAR - 1,)), dma((NEAR - 1,)),
            dma((FAR - 1,)), dma((FAR - 1,)),
            dma((FAR - 1,)), dma((FAR - 1,)),
            dma((NEAR - 1,)), dma((NEAR - 1,)),
        ],
        compiler_params=pltpu.CompilerParams(collective_id=1, has_side_effects=True),
        name="reduce_grads",
    )(rows, payload, wl, wr)


def shards(
    bin_features,
    left_weight,
    right_weight,
    kernel_one,
    kernel_two,
    out_weight,
    dilations,
    band_width,
    tile_table,
    cotangent,
):
    left_t = left_weight.T
    right_t = right_weight.T
    feats = gather_call(bin_features)
    rows, payload = tile_call(
        dilations, band_width, tile_table, feats, left_t, right_t,
        kernel_one, kernel_two, out_weight.reshape(1, CHAN), cotangent,
    )
    bin_grads, left, right, kern, out = reduce_call(rows, payload, left_t, right_t)
    return (bin_grads, left.T, right.T, kern, out.reshape(CHAN))


def solution(mesh):
    placed = (
        P(("pos", "diag"), None),
        P(),
        P(),
        P(),
        P(),
        P(),
        P(),
        P(),
        P("pos", None),
        P(("pos", "diag"), None, None),
    )
    return jax.shard_map(
        shards,
        mesh=mesh,
        in_specs=placed,
        out_specs=(P(("pos", "diag"), None), P(), P(), P(), P()),
        check_vma=False,
    )
```

time: 637 us -> 153 us (0.24)
  matrix products: 173 us -> 0 us
  waiting for transfers between devices: 145 us -> 0 us
  Pallas kernels: 0 us -> 142 us
  local copies, waits for them, and re-layouts: 148 us -> 8.8 us
  blocking collectives: 78.3 us -> 0 us
  other arithmetic: 49.6 us -> 0 us
  between operations: 19.7 us -> 1.45 us
  loops' own time: 12.9 us -> 0 us
  starting transfers between devices: 7.44 us -> 0 us
    dot_general x183 -> x0, matrix products: 173 us -> none  [the longest x54 56.6 us: conv_kernel_grad(): lax.dot_general(flat_slopes, window.reshape(CHAN, -1), (((1,), (1,)), (()...]
    psum x1 -> x0, waiting for transfers between devices: 143 us -> none  [shards(): lax.psum((kern_acc, left_acc, right_acc, out_acc), ('pos', 'diag'))]
    pallas_call x0 -> x3, Pallas kernels: none -> 142 us  [the longest x1 97.9 us: tile_call(): pl.pallas_call(tile_kernel, out_shape=(jax.ShapeDtypeStruct((feats.shape[...]
    while x195 -> x0, local copies, waits for them, and re-layouts: 140 us -> none
    psum x1 -> x0, blocking collectives: 67.4 us -> none  [shards(): lax.psum((kern_acc, left_acc, right_acc, out_acc), ('pos', 'diag'))]
    convert_element_type x14 -> x0, other arithmetic: 18.6 us -> none  [the longest x3 5.47 us: slot_step(): slope_one = (back_one * silu_slope(first_pre)).astype(jnp.bfloat16)]
    another operation x1 -> x0, loops' own time: 12.9 us -> none  [shards(): lax.scan(slot_step, start, (tile_ids, cotangent))]
    while x6 -> x0, other arithmetic: 12.1 us -> none
  transfers between devices with their start and end apart: 4 -> 0, of which waited for: 2 -> 0; matrix products, arithmetic and copies ran while one was open for 2% -> 0% of each run, Pallas kernels for 0% -> 0%
where the time goes in v1:
time: 153 us; the launch traced here: 152 us
  Pallas kernels  142 us (93%)
  local copies, waits for them, and re-layouts  8.8 us (6%)
    pallas_call x1, Pallas kernels, tile_call(): pl.pallas_call(tile_kernel, out_shape=(jax.ShapeDtypeStruct((feats.shape[...  97.9 us
    pallas_call x1, Pallas kernels, reduce_call(): pl.pallas_call(reduce_kernel, out_shape=(jax.ShapeDtypeStruct((count, fea...  29.3 us
    pallas_call x1, Pallas kernels, gather_call(): pl.pallas_call(gather_kernel, out_shape=jax.ShapeDtypeStruct((2 * members...  14.7 us
    unnamed x33, local copies, waits for them, and re-layouts  8.8 us

profile of v1, /device:TPU:1, one launch (start us, length us, event | category | flops | bytes accessed | tf_op | source)
XLA Modules:
  0.0 152.2 jit_solution(1699488656713657302)
XLA Ops:
  1.3 0.0 copy-start.3
  1.3 0.0 copy-start.4
  1.3 0.0 copy-start.5
  1.3 0.0 copy-start.6
  1.3 0.0 copy-start.8
  1.3 0.0 copy-start.9
  1.3 0.0 copy-start.10
  1.4 14.7 %gather_bins.1.feats = bf16[768,256]{1,0:T(8,128)(2,1)} custom-call(bf16[96,256]{1,0:T(8,128)(2,1)} %own_ref.1), custom_call_target="tpu_custom_call" | custom-call | tf_op jit(solution)/shard_map/gather_bins/pallas_call | solution.py:353
  16.0 0.0 copy-done.3
  16.1 0.0 copy-done.4
  16.1 0.0 copy-done.5
  16.1 0.0 copy-done.6
  16.1 0.0 copy-done.8
  16.1 0.0 copy-done.9
  16.1 0.0 copy-done.10
  16.1 0.0 copy-start
  16.1 1.0 copy-done
  17.1 0.9 copy-done.7
  18.0 97.9 %tile_work.1 = (bf16[768,128]{1,0:T(8,128)(2,1)S(1)}, bf16[1024,128]{1,0:T(8,128)(2,1)S(1)}) custom-call(s32[2]{0:T(128)S(1)} %copy-done.8, s32[1]{0:T(128)S(6)} %copy.20.bandw, s32[1,12]{1,0:T(1,128)S(1)} %copy-done.9, bf16[768,256]{1,0:T(8,128)(2,1)S(1)} %copy-done, bf16[64,256]{1,0:T(8,128)(2,1)S(1)} %bitcast.7, bf16[64,256]{1,0:T(8,128)(2,1)S(1)} %bitcast.9, ...), custom_call_target="tpu_custom_call" | custom-call | tf_op jit(solution)/shard_map/tile_work/pallas_call | solution.py:259
  115.9 0.0 copy-start.1
  116.0 0.7 copy-done.1
  116.6 0.7 copy-done.2
  117.3 29.3 %reduce_grads.1 = (f32[96,256]{1,0:T(8,128)}, f32[64,256]{1,0:T(8,128)}, f32[64,256]{1,0:T(8,128)}, f32[2,9,64,64]{3,2,1,0:T(8,128)}, f32[1,64]{1,0:T(1,128)}) custom-call(bf16[768,128]{1,0:T(8,128)(2,1)} %copy-done.2, bf16[1024,128]{1,0:T(8,128)(2,1)} %copy-done.1, bf16[64,256]{1,0:T(8,128)(2,1)} %bitcast.6, bf16[64,256]{1,0:T(8,128)(2,1)} %bitcast.8), custom_call_target="tpu_custom_call" | custom-call | tf_op jit(solution)/shard_map/reduce_grads/pallas_call | solution.py:485
  146.7 0.0 copy-start.12
  146.7 1.6 %copy.21 = f32[96,256]{1,0:T(8,128)} copy(f32[96,256]{1,0:T(8,128)} %get-tuple-element.24) | data formatting | bytes 196608
  148.2 0.0 copy-done.12
  148.3 0.6 copy.22
  148.9 0.2 copy-done.11
  149.1 0.6 copy.23
  149.7 1.9 %copy.24 = f32[2,9,64,64]{3,2,1,0:T(8,128)} copy(f32[2,9,64,64]{3,2,1,0:T(8,128)} %get-tuple-element.27) | data formatting | bytes 589824
  151.7 0.0 copy-done.13
  151.7 0.5 copy.25
  (4 shorter events, 0.0 us)
Async XLA Ops:
  1.3 14.8 %copy-start.3 = (bf16[9,64,64]{2,1,0:T(8,128)(2,1)S(1)}, bf16[9,64,64]{2,1,0:T(8,128)(2,1)}, u32[]{:S(2)}) copy-start(bf16[9,64,64]{2,1,0:T(8,128)(2,1)} %k1.1) | copy-start | bytes 221188
  1.3 14.8 %copy-start.4 = (bf16[9,64,64]{2,1,0:T(8,128)(2,1)S(1)}, bf16[9,64,64]{2,1,0:T(8,128)(2,1)}, u32[]{:S(2)}) copy-start(bf16[9,64,64]{2,1,0:T(8,128)(2,1)} %k2.1) | copy-start | bytes 221188
  1.3 14.8 %copy-start.5 = (bf16[256,64]{0,1:T(8,128)(2,1)S(1)}, bf16[256,64]{0,1:T(8,128)(2,1)}, u32[]{:S(2)}) copy-start(bf16[256,64]{0,1:T(8,128)(2,1)} %param.11) | copy-start | bytes 98308
  1.3 14.8 %copy-start.6 = (bf16[256,64]{0,1:T(8,128)(2,1)S(1)}, bf16[256,64]{0,1:T(8,128)(2,1)}, u32[]{:S(2)}) copy-start(bf16[256,64]{0,1:T(8,128)(2,1)} %param.12) | copy-start | bytes 98308
  1.3 14.8 %copy-start.8 = (s32[2]{0:T(128)S(1)}, s32[2]{0:T(128)}, u32[]{:S(2)}) copy-start(s32[2]{0:T(128)} %dil.1) | copy-start | bytes 28
  1.3 14.8 %copy-start.9 = (s32[1,12]{1,0:T(1,128)S(1)}, s32[1,12]{1,0:T(1,128)}, u32[]{:S(2)}) copy-start(s32[1,12]{1,0:T(1,128)} %table.1) | copy-start | bytes 148
  1.3 14.8 %copy-start.10 = (bf16[64]{0:T(256)(128)(2,1)S(1)}, bf16[64]{0:T(256)(128)(2,1)}, u32[]{:S(2)}) copy-start(bf16[64]{0:T(256)(128)(2,1)} %param.15) | copy-start | bytes 388
  16.1 1.0 copy-start
  17.1 0.9 copy-start.7
  115.9 0.7 copy-start.1
  116.6 0.7 copy-start.2
  146.7 1.6 %copy-start.12 = (f32[64,256]{1,0:T(8,128)S(1)}, f32[64,256]{1,0:T(8,128)}, u32[]{:S(2)}) copy-start(f32[64,256]{1,0:T(8,128)} %get-tuple-element.15) | copy-start | bytes 196612
  148.3 0.9 copy-start.11
  149.7 1.9 %copy-start.13 = (f32[1,64]{1,0:T(1,128)S(1)}, f32[1,64]{1,0:T(1,128)}, u32[]{:S(2)}) copy-start(f32[1,64]{1,0:T(1,128)} %get-tuple-element.18) | copy-start | bytes 772

commit v2 on v1

v2 whole, which is shorter than its diff:
```python
import jax
import jax.numpy as jnp
from jax import lax
from jax.experimental import pallas as pl
from jax.experimental.pallas import tpu as pltpu
from jax.sharding import PartitionSpec as P

TILE = 128
CHAN = 64
BF = jnp.bfloat16
F32 = jnp.float32
NT = (((1,), (1,)), ((), ()))
ROWS = 8
BLOCKS = TILE // ROWS
STRIDE = TILE + 2 * ROWS
MESH = pl.DeviceIdType.MESH
FAR = 16
PIECE = 8
SHARE = FAR * PIECE
HALF = 4 * SHARE
PAYLOAD = 2 * HALF
EW = F32


def mm(a, b):
    return jnp.dot(a, b, preferred_element_type=F32)


def mm_nt(a, b):
    return lax.dot_general(a, b, NT, preferred_element_type=F32)


def shift_lanes(v, distance):
    lane = lax.broadcasted_iota(jnp.int32, v.shape, 1) + distance
    rolled = pltpu.roll(v, lax.rem(TILE - distance, TILE), 1)
    return jnp.where((lane >= 0) & (lane < TILE), rolled, jnp.zeros_like(v))


def tile_kernel(
    dil, bandw, table, feats, wl, wr, k1, k2, outw, cot,
    rows_out, pay_out,
    rows_acc, wmat, hp, d1, s2p, msk, bvar, gat, rsacc, edge, csacc, gacc, rsm, lsh, rsh, idxr, outh,
    keepb, hnew, snew, lbuf, sbuf, ogacc,
):
    e1 = dil[0]
    e2 = dil[1]
    band = bandw[0]
    n_tiles = cot.shape[0]
    group_bins = feats.shape[0] // 2
    first_bin = lax.axis_index("pos") * group_bins
    total_bins = lax.axis_size("pos") * group_bins
    first_slot = lax.axis_index("diag") * n_tiles
    lane = lax.broadcasted_iota(jnp.int32, (CHAN, TILE), 1)
    lane8 = lax.broadcasted_iota(jnp.int32, (8, TILE), 1)

    for which, ref in ((0, k1), (1, k2)):
        wide = ref[...].astype(F32)
        w = jnp.concatenate(
            [jnp.concatenate([wide[3 * q + p] for q in range(3)], axis=1) for p in range(3)], axis=0
        )
        v = jnp.concatenate(
            [jnp.concatenate([wide[3 * p + q] for q in range(3)], axis=1) for p in range(3)], axis=0
        )
        if which == 0:
            wmat[0] = (w * 0.5).astype(BF)
            wmat[1] = (v * 0.5).astype(BF)
            wmat[2] = w.T.astype(BF)
            wmat[3] = v.T.astype(BF)
        else:
            wmat[4] = (w * 0.5).astype(BF)
            wmat[5] = (v.T * 0.5).astype(BF)

    rows_acc[...] = jnp.zeros_like(rows_acc)
    gacc[...] = jnp.zeros_like(gacc)
    csacc[...] = jnp.zeros_like(csacc)
    ogacc[...] = jnp.zeros_like(ogacc)
    for ref in (hnew, snew, lbuf, sbuf):
        ref[...] = jnp.zeros_like(ref)
    zero_rows = jnp.zeros((ROWS, CHAN, TILE), BF)
    for ref in (hp, s2p):
        for t in range(n_tiles + 1):
            ref[t, 0:ROWS] = zero_rows
            ref[t, ROWS + TILE:] = zero_rows
        for b in range(BLOCKS - 8, BLOCKS):
            ref[n_tiles, ROWS + b * ROWS:2 * ROWS + b * ROWS] = zero_rows
    for b in range(BLOCKS - 8, BLOCKS):
        d1[n_tiles, b * ROWS:b * ROWS + ROWS] = zero_rows
    gat[n_tiles] = jnp.zeros((4, CHAN, TILE), F32)
    bvar[n_tiles] = jnp.zeros((3, CHAN, TILE), F32)
    msk[n_tiles] = jnp.zeros((TILE, TILE), F32)
    yy = lax.broadcasted_iota(jnp.int32, (2 * TILE, TILE), 0)
    nn = lax.broadcasted_iota(jnp.int32, (2 * TILE, TILE), 1)
    shifted = yy % TILE + ((nn % 48) // 16 - 1) * e1
    keep = (shifted >= 0) & (shifted < TILE) & (nn < 96) & (nn // 48 == yy // TILE)
    rsm[...] = jnp.where(keep, 1.0, 0.0).astype(BF)
    idxr[...] = jnp.where(lane8 < e1, 32, jnp.where(lane8 >= TILE - e1, 64, 0))
    outh[...] = (jnp.broadcast_to(outw[...].astype(F32), (TILE, CHAN)).T * 0.5).astype(EW)
    lane16 = lane % 16
    low = lane < TILE - e2
    high = lane >= e2
    keepb[0] = jnp.where(high, 1.0, 0.0).astype(BF)
    keepb[1] = jnp.where(low, 1.0, 0.0).astype(BF)

    def stack3(v, step):
        return jnp.concatenate([shift_lanes(v, -step), v, shift_lanes(v, step)], axis=0)

    places = []
    for t in range(n_tiles):
        tid = table[0, first_slot + t]
        upper = lax.div(tid, 4)
        lower = upper + lax.rem(tid, 4)
        upper_at = pl.multiple_of(upper * TILE, TILE)
        lower_at = pl.multiple_of(lower * TILE, TILE)
        places.append((upper_at, lower_at))
        left = mm_nt(wl[...], feats[pl.ds(upper_at, TILE), :]).astype(BF).astype(F32)
        right = mm_nt(wr[...], feats[pl.ds(lower_at, TILE), :]).astype(BF).astype(F32)
        left3 = stack3(left, e1).astype(BF)
        right3 = stack3(right, e1).astype(BF)
        lsh[t] = left3
        rsh[t] = right3
        a_out = mm(wmat[0], left3)
        b_out = mm(wmat[1], right3)
        am, a0, ap = a_out[0:64], a_out[64:128], a_out[128:192]
        bm, b0, bp = b_out[0:64], b_out[64:128], b_out[128:192]
        bvar[t, 0] = bm + b0 + bp
        bvar[t, 1] = b0 + bp
        bvar[t, 2] = bm + b0
        variants = (am + a0 + ap, a0 + ap, am + a0)
        for k in range(4):
            gat[t, k] = jnp.concatenate(
                [va[:, 32 * k:32 * k + 32] for va in variants] + [jnp.zeros((CHAN, 32), F32)], axis=1
            )
        xx = lax.broadcasted_iota(jnp.int32, (TILE, TILE), 0)
        y2 = lax.broadcasted_iota(jnp.int32, (TILE, TILE), 1)
        gap = (lower - upper) * TILE + y2 - xx
        inside = (gap >= 0) & (gap <= band) & (first_bin + lower * TILE + y2 < total_bins)
        msk[t] = jnp.where(inside, cot[t].astype(F32), 0.0)

    def taps(ref, t, x, spread):
        return jnp.concatenate(
            [ref[t, x + ROWS - spread], ref[t, x + ROWS], ref[t, x + ROWS + spread]], axis=0
        )

    def where_is(i):
        i = jnp.where(i < 0, i + (n_tiles + 1) * BLOCKS, i)
        return lax.div(i, BLOCKS), lax.rem(i, BLOCKS)

    def roll16(v, which):
        amount = e2 if which == 0 else TILE - e2
        return pltpu.roll(v, amount, 1) * keepb[which]

    def all_taps(ref, t, blk, spread):
        return jnp.concatenate(
            [taps(ref, t, blk * ROWS + j, spread) for j in range(ROWS)], axis=1
        )

    def settle(i, par):
        t, blk = where_is(i - 1)
        for j in range(ROWS):
            hp[t, blk * ROWS + j + ROWS] = hnew[1 - par, j]
        t, blk = where_is(i - 4)
        for j in range(ROWS):
            s2p[t, blk * ROWS + j + ROWS] = snew[par, j]

    def kernel_grad(i, par):
        t, blk = where_is(i)
        gacc[...] += mm_nt(lbuf[par], all_taps(hp, t, blk, e2))

    def row_sums(i, par):
        t, blk = where_is(i)
        quarter = lax.div(blk, 4)
        sums = mm(sbuf[par], rsm[...])
        acc = rsacc[t, quarter]
        for p in range(ROWS // 2):
            acc = jnp.where(lane16 == lax.rem(blk, 4) * 4 + p, sums[CHAN * p:CHAN * p + CHAN], acc)
        rsacc[t, quarter] = acc

    def phase_one(i, par):
        t, blk = where_is(i)
        values = gat[t, lax.div(blk, 4)]
        base = idxr[...] + lax.rem(blk, 4) * ROWS
        for j in range(ROWS):
            x = blk * ROWS + j
            kind = jnp.where(x < e1, 1, jnp.where(x >= TILE - e1, 2, 0))
            at = base + j
            u = jnp.concatenate(
                [
                    jnp.take_along_axis(values[8 * g:8 * g + 8], at, axis=1, mode="promise_in_bounds")
                    for g in range(CHAN // 8)
                ],
                axis=0,
            )
            u = (u + bvar[t, kind]).astype(EW)
            th = jnp.tanh(u)
            w = u * th
            hnew[par, j] = (u + w).astype(BF)
            d1[t, x] = ((1.0 + th) * ((1.0 + u) - w)).astype(BF)

    def phase_two(i, par, z):
        t, blk = where_is(i)
        og = ogacc[...]
        for j in range(ROWS):
            cols = z[:, j * TILE:(j + 1) * TILE]
            sides = roll16(cols[0:64].astype(BF), 0) + roll16(cols[128:192].astype(BF), 1)
            u = cols[64:128] + sides.astype(F32)
            th = jnp.tanh(u)
            w = u * th
            m = msk[t, pl.ds(blk * ROWS + j, 1), :]
            og = og + (u + w) * m
            s = ((outh[...] * m) * ((1.0 + th) * ((1.0 + u) - w))).astype(BF)
            snew[par, j] = s
            lbuf[par, 0:64, j * TILE:(j + 1) * TILE] = roll16(s, 1)
            lbuf[par, 64:128, j * TILE:(j + 1) * TILE] = s
            lbuf[par, 128:192, j * TILE:(j + 1) * TILE] = roll16(s, 0)
        ogacc[...] = og

    def phase_three(i, par, z):
        t, blk = where_is(i)
        slot = jnp.where(blk == 0, 0, jnp.where(blk == BLOCKS - 1, 1, 2))
        slopes = []
        for j in range(ROWS):
            cols = z[:, j * TILE:(j + 1) * TILE]
            sides = roll16(cols[0:64].astype(BF), 1) + roll16(cols[128:192].astype(BF), 0)
            back = cols[64:128] + sides.astype(F32)
            s = back * d1[t, blk * ROWS + j].astype(F32)
            slopes.append(s)
            s = s.astype(BF)
            edge[t, slot, j] = s
            p, q = j // 2, j % 2
            sbuf[par, CHAN * p:CHAN * p + CHAN, TILE * q:TILE * q + TILE] = s
        while len(slopes) > 1:
            slopes = [slopes[k] + slopes[k + 1] for k in range(0, len(slopes), 2)]
        csacc[t] += slopes[0]

    def step(i, par):
        settle(i, par)
        t, blk = where_is(i - 5)
        z3 = mm(wmat[5], all_taps(s2p, t, blk, -e2))
        t, blk = where_is(i - 2)
        z2 = mm(wmat[4], all_taps(hp, t, blk, e2))
        kernel_grad(i - 4, par)
        row_sums(i - 7, par)
        phase_one(i, par)
        phase_three(i - 5, par, z3)
        phase_two(i - 2, par, z2)

    def two_steps(n, carry):
        step(2 * n, 0)
        step(2 * n + 1, 1)
        return carry

    lax.fori_loop(0, (n_tiles * BLOCKS + 8) // 2, two_steps, 0)

    k1a = jnp.zeros((192, 192), F32)
    k1b = jnp.zeros((192, 192), F32)
    lg_acc = jnp.zeros((CHAN, feats.shape[1]), F32)
    rg_acc = jnp.zeros((CHAN, feats.shape[1]), F32)
    left_half = lax.broadcasted_iota(jnp.int32, (TILE, TILE), 1) < CHAN
    for t in range(n_tiles):
        upper_at, lower_at = places[t]
        sums = []
        for b in range(3):
            pick = lane % 2 * 48 + 16 * b + lane % 32 // 2
            got = None
            for k in range(4):
                part = jnp.take_along_axis(rsacc[t, k], pick, axis=1, mode="promise_in_bounds")
                got = part if got is None else jnp.where(lane // 32 == k, part, got)
            sums.append(got)
        rs16 = jnp.concatenate(sums, axis=0).astype(BF)
        cs0 = csacc[t]
        head = jnp.zeros((CHAN, TILE), F32)
        tail = jnp.zeros((CHAN, TILE), F32)
        for j in range(ROWS):
            head = head + jnp.where(j < e1, edge[t, 0, j].astype(F32), 0.0)
            tail = tail + jnp.where(j >= ROWS - e1, edge[t, 1, j].astype(F32), 0.0)
        cs16 = jnp.concatenate([cs0 - head, cs0, cs0 - tail], axis=0).astype(BF)
        k1a = k1a + mm_nt(rs16, lsh[t])
        k1b = k1b + mm_nt(cs16, rsh[t])
        yl = mm(wmat[2], rs16)
        yr = mm(wmat[3], cs16)
        lg = yl[64:128] + shift_lanes(yl[0:64], e1) + shift_lanes(yl[128:192], -e1)
        rg = yr[64:128] + shift_lanes(yr[0:64], e1) + shift_lanes(yr[128:192], -e1)
        lg_acc = lg_acc + mm(lg.astype(BF), feats[pl.ds(upper_at, TILE), :])
        rg_acc = rg_acc + mm(rg.astype(BF), feats[pl.ds(lower_at, TILE), :])
        both = jnp.concatenate([lg, rg], axis=0).T
        rows_acc[pl.ds(upper_at, TILE), :] += jnp.where(left_half, both, 0.0)
        rows_acc[pl.ds(lower_at, TILE), :] += jnp.where(left_half, 0.0, both)

    for a in range(3):
        for b in range(3):
            tap = 3 * a + b
            one = (
                k1a[64 * b:64 * b + 64, 64 * a:64 * a + 64]
                + k1b[64 * a:64 * a + 64, 64 * b:64 * b + 64]
            )
            two = gacc[64 * b:64 * b + 64, 64 * a:64 * a + 64]
            pay_out[64 * tap:64 * tap + 64] = jnp.concatenate([one, two], axis=1).astype(BF)
    grads = jnp.concatenate([lg_acc, rg_acc], axis=0)
    pay_out[576:704] = grads[:, 0:TILE].astype(BF)
    pay_out[704:832] = grads[:, TILE:2 * TILE].astype(BF)
    out_sum = jnp.sum(ogacc[...], axis=1, keepdims=True)
    out_row = jnp.concatenate(
        [jnp.broadcast_to(out_sum, (CHAN, TILE)), jnp.zeros((TILE - CHAN, TILE), F32)], axis=0
    ).T[0:16]
    pay_out[832:848] = out_row.astype(BF)
    pay_out[848:] = jnp.zeros((PAYLOAD - 848, TILE), BF)
    rows_out[...] = rows_acc[...].astype(BF)


def tile_call(dilations, band_width, tile_table, feats, wl, wr, k1, k2, outw, cot):
    vm = pl.BlockSpec(memory_space=pltpu.VMEM)
    sm = pl.BlockSpec(memory_space=pltpu.SMEM)
    n = cot.shape[0]
    return pl.pallas_call(
        tile_kernel,
        out_shape=(
            jax.ShapeDtypeStruct((feats.shape[0], 2 * CHAN), BF),
            jax.ShapeDtypeStruct((PAYLOAD, TILE), BF),
        ),
        in_specs=[sm] * 3 + [vm] * 7,
        out_specs=(vm, vm),
        scratch_shapes=[
            pltpu.VMEM((feats.shape[0], 2 * CHAN), F32),
            pltpu.VMEM((6, 192, 192), BF),
            pltpu.VMEM((n + 1, STRIDE, CHAN, TILE), BF),
            pltpu.VMEM((n + 1, TILE, CHAN, TILE), BF),
            pltpu.VMEM((n + 1, STRIDE, CHAN, TILE), BF),
            pltpu.VMEM((n + 1, TILE, TILE), F32),
            pltpu.VMEM((n + 1, 3, CHAN, TILE), F32),
            pltpu.VMEM((n + 1, 4, CHAN, TILE), F32),
            pltpu.VMEM((n + 1, 4, CHAN, TILE), F32),
            pltpu.VMEM((n + 1, 3, ROWS, CHAN, TILE), BF),
            pltpu.VMEM((n + 1, CHAN, TILE), F32),
            pltpu.VMEM((192, 192), F32),
            pltpu.VMEM((2 * TILE, TILE), BF),
            pltpu.VMEM((n, 192, TILE), BF),
            pltpu.VMEM((n, 192, TILE), BF),
            pltpu.VMEM((8, TILE), jnp.int32),
            pltpu.VMEM((CHAN, TILE), EW),
            pltpu.VMEM((2, CHAN, TILE), BF),
            pltpu.VMEM((2, ROWS, CHAN, TILE), BF),
            pltpu.VMEM((2, ROWS, CHAN, TILE), BF),
            pltpu.VMEM((2, 192, ROWS * TILE), BF),
            pltpu.VMEM((2, ROWS // 2 * CHAN, 2 * TILE), BF),
            pltpu.VMEM((CHAN, TILE), F32),
        ],
        compiler_params=pltpu.CompilerParams(vmem_limit_bytes=50 * 1024 * 1024),
        name="tile_work",
    )(dilations, band_width, tile_table, feats, wl, wr, k1, k2, outw, cot)


def greet(devices):
    barrier = pltpu.get_barrier_semaphore()
    for device in devices:
        pl.semaphore_signal(barrier, inc=1, device_id=device, device_id_type=MESH)
    pl.semaphore_wait(barrier, len(devices))


def remote(src, dst, send, recv, device):
    return pltpu.make_async_remote_copy(
        src_ref=src, dst_ref=dst, send_sem=send, recv_sem=recv, device_id=device, device_id_type=MESH
    )


def gather_kernel(own_ref, all_ref, send, recv):
    ranges = lax.axis_size("pos")
    members = lax.axis_size("diag")
    pos = lax.axis_index("pos")
    diag = lax.axis_index("diag")
    rows = own_ref.shape[0]
    half = members * rows
    before = (lax.rem(pos + ranges - 1, ranges), diag)
    after = (lax.rem(pos + 1, ranges), diag)
    others = [(pos, lax.rem(diag + k, members)) for k in range(1, members)]
    greet(others + [before, after])

    def place(owner, base):
        return pl.ds(pl.multiple_of(base + owner * rows, 32), rows)

    all_ref[place(diag, 0), :] = own_ref[...]
    copies = []
    first = remote(own_ref, all_ref.at[place(diag, half)], send.at[0], recv.at[0], before)
    first.start()
    for k in range(1, members):
        copy = remote(own_ref, all_ref.at[place(diag, 0)], send.at[k], recv.at[k], others[k - 1])
        copy.start()
        copies.append(copy)
    passed = []
    for k in (1, 3, 2):
        copies[k - 1].wait_recv()
        owner = lax.rem(diag + members - k, members)
        copy = remote(
            all_ref.at[place(owner, 0)],
            all_ref.at[place(owner, half)],
            send.at[members + k - 1],
            recv.at[members + k - 1],
            before,
        )
        copy.start()
        passed.append(copy)
    for copy in copies:
        copy.wait_send()
    first.wait()
    for copy in passed:
        copy.wait()


def gather_call(own):
    vm = pl.BlockSpec(memory_space=pltpu.VMEM)
    members = lax.axis_size("diag")
    return pl.pallas_call(
        gather_kernel,
        out_shape=jax.ShapeDtypeStruct((2 * members * own.shape[0], own.shape[1]), own.dtype),
        in_specs=[vm],
        out_specs=vm,
        scratch_shapes=[
            pltpu.SemaphoreType.DMA((2 * members,)),
            pltpu.SemaphoreType.DMA((2 * members,)),
        ],
        compiler_params=pltpu.CompilerParams(collective_id=0, has_side_effects=True),
        name="gather_bins",
    )(own)


def reduce_kernel(
    rows_ref, pay_ref,
    rows_out, all_out,
    row_buf, core_buf, half_sum, near_buf, near_sum, far_buf, far_all, near_own,
    row_send, row_recv, core_send, core_recv, near_send, near_recv, far_send, far_recv,
    back_send, back_recv, last_send, last_recv, pass_send, pass_recv,
):
    ranges = lax.axis_size("pos")
    members = lax.axis_size("diag")
    pos = lax.axis_index("pos")
    diag = lax.axis_index("diag")
    core = lax.rem(pos, 2)
    chip = lax.div(pos, 2)
    count = rows_out.shape[0]
    half = members * count
    after = lax.rem(pos + 1, ranges)
    across = lax.rem(pos + ranges + 2 * core - 1, ranges)
    sibling = (2 * chip + 1 - core, diag)

    diag_ids = [lax.rem(diag + k, members) for k in range(1, members)]
    diag_devs = [(pos, d) for d in diag_ids]
    far_ids = [lax.rem(chip + k, FAR) for k in range(1, FAR)]
    far_devs = [(2 * f + core, diag) for f in far_ids]
    greet(
        [(2 * chip + 1 - core, d) for d in range(members)]
        + diag_devs
        + far_devs
        + [(across, d) for d in range(members)]
    )

    def piece(index, size):
        return pl.ds(pl.multiple_of(index * size, size), size)

    core_copy = remote(
        pay_ref.at[piece(1 - core, HALF)], core_buf, core_send.at[0], core_recv.at[0], sibling
    )
    core_copy.start()
    core_copy.wait_recv()
    half_sum[...] = (pay_ref[piece(core, HALF), :].astype(F32) + core_buf[...].astype(F32)).astype(BF)
    near_copies = []
    for k in range(1, members):
        copy = remote(
            half_sum.at[piece(diag_ids[k - 1], SHARE)], near_buf.at[k - 1],
            near_send.at[k - 1], near_recv.at[k - 1], diag_devs[k - 1],
        )
        copy.start()
        near_copies.append(copy)
    total = half_sum[piece(diag, SHARE), :].astype(F32)
    for k in range(1, members):
        near_copies[k - 1].wait_recv()
        total = total + near_buf[k - 1].astype(F32)
    near_sum[...] = total
    far_copies = []
    for k in range(1, FAR):
        copy = remote(
            near_sum.at[piece(far_ids[k - 1], PIECE)], far_buf.at[k - 1],
            far_send.at[k - 1], far_recv.at[k - 1], far_devs[k - 1],
        )
        copy.start()
        far_copies.append(copy)
    row_copies = []
    for k in range(1, 2 * members):
        owner = lax.rem(diag + k, members)
        base = 0 if k < members else half
        target = (pos, owner) if k < members else (after, owner)
        copy = remote(
            rows_ref.at[pl.ds(pl.multiple_of(base + owner * count, 32), count)], row_buf.at[k - 1],
            row_send.at[k - 1], row_recv.at[k - 1], target,
        )
        copy.start()
        row_copies.append(copy)

    mine = near_sum[piece(chip, PIECE), :]
    for k in range(1, FAR):
        far_copies[k - 1].wait_recv()
        mine = mine + far_buf[k - 1]
    far_all[piece(chip, PIECE), :] = mine * (1.0 / ranges)
    back_copies = []
    for k in range(1, FAR):
        copy = remote(
            far_all.at[piece(chip, PIECE)], far_all.at[piece(chip, PIECE)],
            back_send.at[k - 1], back_recv.at[k - 1], far_devs[k - 1],
        )
        copy.start()
        back_copies.append(copy)

    rows = rows_ref[pl.ds(pl.multiple_of(diag * count, 32), count), :].astype(F32)
    for k in range(1, 2 * members):
        row_copies[k - 1].wait_recv()
        rows = rows + row_buf[k - 1].astype(F32)
    rows_out[...] = rows.astype(BF)

    for k in range(1, FAR):
        back_copies[k - 1].wait_recv()
    near_own[...] = far_all[...].astype(BF)

    def spot(owner):
        return pl.ds(pl.multiple_of(core * HALF + owner * SHARE, SHARE), SHARE)

    last_copies = []
    for k in range(1, members):
        copy = remote(
            near_own, all_out.at[spot(diag)],
            last_send.at[k - 1], last_recv.at[k - 1], diag_devs[k - 1],
        )
        copy.start()
        last_copies.append(copy)
    pass_copies = [
        remote(near_own, all_out.at[spot(diag)], pass_send.at[0], pass_recv.at[0], sibling)
    ]
    pass_copies[0].start()
    all_out[spot(diag), :] = near_own[...]
    for k in (1, 3, 2):
        last_copies[k - 1].wait_recv()
        owner = lax.rem(diag + members - k, members)
        copy = remote(
            all_out.at[spot(owner)], all_out.at[spot(owner)], pass_send.at[k], pass_recv.at[k], sibling
        )
        copy.start()
        pass_copies.append(copy)
    for copy in pass_copies:
        copy.wait_recv()
    for copy in [core_copy] + near_copies + row_copies + far_copies + back_copies + last_copies + pass_copies:
        copy.wait_send()


def reduce_call(rows, payload):
    vm = pl.BlockSpec(memory_space=pltpu.VMEM)
    members = lax.axis_size("diag")
    count = rows.shape[0] // (2 * members)
    dma = pltpu.SemaphoreType.DMA
    return pl.pallas_call(
        reduce_kernel,
        out_shape=(
            jax.ShapeDtypeStruct((count, 2 * CHAN), BF),
            jax.ShapeDtypeStruct((PAYLOAD, TILE), BF),
        ),
        in_specs=[vm] * 2,
        out_specs=(vm,) * 2,
        scratch_shapes=[
            pltpu.VMEM((2 * members - 1, count, 2 * CHAN), BF),
            pltpu.VMEM((HALF, TILE), BF),
            pltpu.VMEM((HALF, TILE), BF),
            pltpu.VMEM((members - 1, SHARE, TILE), BF),
            pltpu.VMEM((SHARE, TILE), F32),
            pltpu.VMEM((FAR - 1, PIECE, TILE), F32),
            pltpu.VMEM((SHARE, TILE), F32),
            pltpu.VMEM((SHARE, TILE), BF),
            dma((2 * members - 1,)), dma((2 * members - 1,)),
            dma((1,)), dma((1,)),
            dma((members - 1,)), dma((members - 1,)),
            dma((FAR - 1,)), dma((FAR - 1,)),
            dma((FAR - 1,)), dma((FAR - 1,)),
            dma((members - 1,)), dma((members - 1,)),
            dma((members,)), dma((members,)),
        ],
        compiler_params=pltpu.CompilerParams(collective_id=1, has_side_effects=True),
        name="reduce_grads",
    )(rows, payload)


def finish_kernel(rows, sums, wl, wr, bin_out, left_out, right_out, kern_out, out_out):
    weights = jnp.concatenate([wl[...], wr[...]], axis=0)
    bin_out[...] = mm(rows[...], weights)
    for tap in range(9):
        block = sums[64 * tap:64 * tap + 64, :].astype(F32)
        kern_out[0, tap] = block[:, 0:CHAN]
        kern_out[1, tap] = block[:, CHAN:2 * CHAN]
    for part in range(2):
        block = sums[576 + TILE * part:576 + TILE * part + TILE, :].astype(F32)
        left_out[:, TILE * part:TILE * part + TILE] = block[0:CHAN]
        right_out[:, TILE * part:TILE * part + TILE] = block[CHAN:2 * CHAN]
    out_out[...] = sums[832:848, :].astype(F32)[0:1, 0:CHAN]


def finish_call(rows, sums, wl, wr):
    vm = pl.BlockSpec(memory_space=pltpu.VMEM)
    feat = wl.shape[1]
    return pl.pallas_call(
        finish_kernel,
        out_shape=(
            jax.ShapeDtypeStruct((rows.shape[0], feat), F32),
            jax.ShapeDtypeStruct((CHAN, feat), F32),
            jax.ShapeDtypeStruct((CHAN, feat), F32),
            jax.ShapeDtypeStruct((2, 9, CHAN, CHAN), F32),
            jax.ShapeDtypeStruct((1, CHAN), F32),
        ),
        in_specs=[vm] * 4,
        out_specs=(vm,) * 5,
        name="finish",
    )(rows, sums, wl, wr)


def shards(
    bin_features,
    left_weight,
    right_weight,
    kernel_one,
    kernel_two,
    out_weight,
    dilations,
    band_width,
    tile_table,
    cotangent,
):
    left_t = left_weight.T
    right_t = right_weight.T
    feats = gather_call(bin_features)
    rows, payload = tile_call(
        dilations, band_width, tile_table, feats, left_t, right_t,
        kernel_one, kernel_two, out_weight.reshape(1, CHAN), cotangent,
    )
    rows, sums = reduce_call(rows, payload)
    bin_grads, left, right, kern, out = finish_call(rows, sums, left_t, right_t)
    return (bin_grads, left.T, right.T, kern, out.reshape(CHAN))


def solution(mesh):
    placed = (
        P(("pos", "diag"), None),
        P(),
        P(),
        P(),
        P(),
        P(),
        P(),
        P(),
        P("pos", None),
        P(("pos", "diag"), None, None),
    )
    return jax.shard_map(
        shards,
        mesh=mesh,
        in_specs=placed,
        out_specs=(P(("pos", "diag"), None), P(), P(), P(), P()),
        check_vma=False,
    )
```

time: 153 us -> 87 us (0.57)
  Pallas kernels: 142 us -> 82.1 us
  local copies, waits for them, and re-layouts: 8.8 us -> 3.29 us
    pallas_call x1, Pallas kernels: 97.9 us -> 36 us  [tile_call(): pl.pallas_call(tile_kernel, out_shape=(jax.ShapeDtypeStruct((feats.shape[...]
    unnamed x33 -> x22, local copies, waits for them, and re-layouts: 8.8 us -> 3.29 us
    pallas_call x1 -> x2, Pallas kernels: 29.3 us -> 31.4 us  [the longest x1 29.5 us: reduce_call(): pl.pallas_call(reduce_kernel, out_shape=(jax.ShapeDtypeStruct((count, 2 *...]
where the time goes in v2:
time: 87 us; the launch traced here: 86.8 us
  Pallas kernels  82.1 us (94%)
  local copies, waits for them, and re-layouts  3.29 us (4%)
  between operations  1.43 us (2%)
    pallas_call x1, Pallas kernels, tile_call(): pl.pallas_call(tile_kernel, out_shape=(jax.ShapeDtypeStruct((feats.shape[...  36 us
    pallas_call x1, Pallas kernels, reduce_call(): pl.pallas_call(reduce_kernel, out_shape=(jax.ShapeDtypeStruct((count, 2 *...  29.5 us
    pallas_call x1, Pallas kernels, gather_call(): pl.pallas_call(gather_kernel, out_shape=jax.ShapeDtypeStruct((2 * members...  14.7 us
    unnamed x22, local copies, waits for them, and re-layouts  3.29 us
    pallas_call x1, Pallas kernels, finish_call(): pl.pallas_call(finish_kernel, out_shape=(jax.ShapeDtypeStruct((rows.shape...  1.93 us

profile of v2, /device:TPU:1, one launch (start us, length us, event | category | flops | bytes accessed | tf_op | source)
XLA Modules:
  0.0 86.8 jit_solution(4323973785726693432)
XLA Ops:
  1.3 0.0 copy-start.3
  1.3 0.0 copy-start.4
  1.3 0.0 copy-start.5
  1.3 0.0 copy-start.6
  1.3 0.0 copy-start.8
  1.3 0.0 copy-start.9
  1.3 0.0 copy-start.10
  1.4 14.7 %gather_bins.1.feats = bf16[768,256]{1,0:T(8,128)(2,1)} custom-call(bf16[96,256]{1,0:T(8,128)(2,1)} %own_ref.1), custom_call_target="tpu_custom_call" | custom-call | tf_op jit(solution)/shard_map/gather_bins/pallas_call | solution.py:411
  16.0 0.0 copy-done.3
  16.1 0.0 copy-done.4
  16.1 0.0 copy-done.5
  16.1 0.0 copy-done.6
  16.1 0.0 copy-done.8
  16.1 0.0 copy-done.9
  16.1 0.0 copy-done.10
  16.1 0.0 copy-start
  16.1 1.0 %copy-done = bf16[768,256]{1,0:T(8,128)(2,1)S(1)} copy-done((bf16[768,256]{1,0:T(8,128)(2,1)S(1)}, bf16[768,256]{1,0:T(8,128)(2,1)}, u32[]{:S(2)}) %copy-start) | copy-done | bytes 393240
  17.1 0.0 copy-start.7
  17.1 0.9 %copy-done.7 = bf16[3,128,128]{2,1,0:T(8,128)(2,1)S(1)} copy-done((bf16[3,128,128]{2,1,0:T(8,128)(2,1)S(1)}, bf16[3,128,128]{2,1,0:T(8,128)(2,1)}, u32[]{:S(2)}) %copy-start.7) | copy-done | bytes 98328
  18.0 36.0 %tile_work.1 = (bf16[768,128]{1,0:T(8,128)(2,1)S(1)}, bf16[1024,128]{1,0:T(8,128)(2,1)S(1)}) custom-call(s32[2]{0:T(128)S(1)} %copy-done.8, s32[1]{0:T(128)S(6)} %copy.15.bandw, s32[1,12]{1,0:T(1,128)S(1)} %copy-done.9, bf16[768,256]{1,0:T(8,128)(2,1)S(1)} %copy-done, bf16[64,256]{1,0:T(8,128)(2,1)S(1)} %bitcast.7, bf16[64,256]{1,0:T(8,128)(2,1)S(1)} %bitcast.9, ...), custom_call_target="tpu_custom_call" | custom-call | tf_op jit(solution)/shard_map/tile_work/pallas_call | solution.py:314
  54.0 0.0 copy-start.1
  54.0 0.7 copy-done.1
  54.7 0.0 copy-start.2
  54.7 0.7 copy-done.2
  55.4 29.5 %reduce_grads.1 = (bf16[96,128]{1,0:T(8,128)(2,1)}, bf16[1024,128]{1,0:T(8,128)(2,1)}) custom-call(bf16[768,128]{1,0:T(8,128)(2,1)} %copy-done.2, bf16[1024,128]{1,0:T(8,128)(2,1)} %copy-done.1), custom_call_target="tpu_custom_call" | custom-call | tf_op jit(solution)/shard_map/reduce_grads/pallas_call | solution.py:556
  84.9 1.9 %finish.1 = (f32[96,256]{1,0:T(8,128)}, f32[64,256]{1,0:T(8,128)}, f32[64,256]{1,0:T(8,128)}, f32[2,9,64,64]{3,2,1,0:T(8,128)}, f32[1,64]{1,0:T(1,128)}) custom-call(bf16[96,128]{1,0:T(8,128)(2,1)} %get-tuple-element.16.rows, bf16[1024,128]{1,0:T(8,128)(2,1)} %get-tuple-element.17.sums, bf16[64,256]{1,0:T(8,128)(2,1)} %bitcast.6, bf16[64,256]{1,0:T(8,128)(2,1)} %bitcast.8), custom_call_target="tpu_custom_call" | custom-call | tf_op jit(solution)/shard_map/finish/pallas_call | solution.py:603
Async XLA Ops:
  1.3 14.8 %copy-start.3 = (bf16[9,64,64]{2,1,0:T(8,128)(2,1)S(1)}, bf16[9,64,64]{2,1,0:T(8,128)(2,1)}, u32[]{:S(2)}) copy-start(bf16[9,64,64]{2,1,0:T(8,128)(2,1)} %k1.1) | copy-start | bytes 221188
  1.3 14.8 %copy-start.4 = (bf16[9,64,64]{2,1,0:T(8,128)(2,1)S(1)}, bf16[9,64,64]{2,1,0:T(8,128)(2,1)}, u32[]{:S(2)}) copy-start(bf16[9,64,64]{2,1,0:T(8,128)(2,1)} %k2.1) | copy-start | bytes 221188
  1.3 14.8 %copy-start.5 = (bf16[256,64]{0,1:T(8,128)(2,1)S(1)}, bf16[256,64]{0,1:T(8,128)(2,1)}, u32[]{:S(2)}) copy-start(bf16[256,64]{0,1:T(8,128)(2,1)} %param.11) | copy-start | bytes 98308
  1.3 14.8 %copy-start.6 = (bf16[256,64]{0,1:T(8,128)(2,1)S(1)}, bf16[256,64]{0,1:T(8,128)(2,1)}, u32[]{:S(2)}) copy-start(bf16[256,64]{0,1:T(8,128)(2,1)} %param.12) | copy-start | bytes 98308
  1.3 14.8 %copy-start.8 = (s32[2]{0:T(128)S(1)}, s32[2]{0:T(128)}, u32[]{:S(2)}) copy-start(s32[2]{0:T(128)} %dil.1) | copy-start | bytes 28
  1.3 14.8 %copy-start.9 = (s32[1,12]{1,0:T(1,128)S(1)}, s32[1,12]{1,0:T(1,128)}, u32[]{:S(2)}) copy-start(s32[1,12]{1,0:T(1,128)} %table.1) | copy-start | bytes 148
  1.3 14.8 %copy-start.10 = (bf16[64]{0:T(256)(128)(2,1)S(1)}, bf16[64]{0:T(256)(128)(2,1)}, u32[]{:S(2)}) copy-start(bf16[64]{0:T(256)(128)(2,1)} %param.15) | copy-start | bytes 388
  16.1 1.0 %copy-start = (bf16[768,256]{1,0:T(8,128)(2,1)S(1)}, bf16[768,256]{1,0:T(8,128)(2,1)}, u32[]{:S(2)}) copy-start(bf16[768,256]{1,0:T(8,128)(2,1)} %gather_bins.1.feats) | copy-start | bytes 1179652
  17.1 0.9 %copy-start.7 = (bf16[3,128,128]{2,1,0:T(8,128)(2,1)S(1)}, bf16[3,128,128]{2,1,0:T(8,128)(2,1)}, u32[]{:S(2)}) copy-start(bf16[3,128,128]{2,1,0:T(8,128)(2,1)} %cot.1) | copy-start | bytes 294916
  54.0 0.7 copy-start.1
  54.7 0.7 copy-start.2

commit v3 on v2

--- a/solution.py
+++ b/solution.py
@@ -14,12 +14,11 @@
 BLOCKS = TILE // ROWS
 STRIDE = TILE + 2 * ROWS
 MESH = pl.DeviceIdType.MESH
-FAR = 16
-PIECE = 8
-SHARE = FAR * PIECE
-HALF = 4 * SHARE
+THIRD = 144
+HALF = 3 * THIRD
 PAYLOAD = 2 * HALF
 EW = F32
+MIB = 1024 * 1024
 
 
 def mm(a, b):
@@ -40,7 +39,7 @@
     dil, bandw, table, feats, wl, wr, k1, k2, outw, cot,
     rows_out, pay_out,
     rows_acc, wmat, hp, d1, s2p, msk, bvar, gat, rsacc, edge, csacc, gacc, rsm, lsh, rsh, idxr, outh,
-    keepb, hnew, snew, lbuf, sbuf, ogacc,
+    keepb, snew, lbuf, sbuf, ogacc,
 ):
     e1 = dil[0]
     e2 = dil[1]
@@ -68,26 +67,18 @@
             wmat[3] = v.T.astype(BF)
         else:
             wmat[4] = (w * 0.5).astype(BF)
-            wmat[5] = (v.T * 0.5).astype(BF)
+            row = jnp.broadcast_to(outw[...].astype(F32) * 0.5, (192, CHAN))
+            wmat[5] = (v.T * jnp.concatenate([row] * 3, axis=1) * 0.5).astype(BF)
 
     rows_acc[...] = jnp.zeros_like(rows_acc)
     gacc[...] = jnp.zeros_like(gacc)
     csacc[...] = jnp.zeros_like(csacc)
     ogacc[...] = jnp.zeros_like(ogacc)
-    for ref in (hnew, snew, lbuf, sbuf):
-        ref[...] = jnp.zeros_like(ref)
     zero_rows = jnp.zeros((ROWS, CHAN, TILE), BF)
     for ref in (hp, s2p):
-        for t in range(n_tiles + 1):
+        for t in range(n_tiles):
             ref[t, 0:ROWS] = zero_rows
             ref[t, ROWS + TILE:] = zero_rows
-        for b in range(BLOCKS - 8, BLOCKS):
-            ref[n_tiles, ROWS + b * ROWS:2 * ROWS + b * ROWS] = zero_rows
-    for b in range(BLOCKS - 8, BLOCKS):
-        d1[n_tiles, b * ROWS:b * ROWS + ROWS] = zero_rows
-    gat[n_tiles] = jnp.zeros((4, CHAN, TILE), F32)
-    bvar[n_tiles] = jnp.zeros((3, CHAN, TILE), F32)
-    msk[n_tiles] = jnp.zeros((TILE, TILE), F32)
     yy = lax.broadcasted_iota(jnp.int32, (2 * TILE, TILE), 0)
     nn = lax.broadcasted_iota(jnp.int32, (2 * TILE, TILE), 1)
     shifted = yy % TILE + ((nn % 48) // 16 - 1) * e1
@@ -142,7 +133,7 @@
         )
 
     def where_is(i):
-        i = jnp.where(i < 0, i + (n_tiles + 1) * BLOCKS, i)
+        i = jnp.int32(i)
         return lax.div(i, BLOCKS), lax.rem(i, BLOCKS)
 
     def roll16(v, which):
@@ -154,17 +145,21 @@
             [taps(ref, t, blk * ROWS + j, spread) for j in range(ROWS)], axis=1
         )
 
-    def settle(i, par):
-        t, blk = where_is(i - 1)
-        for j in range(ROWS):
-            hp[t, blk * ROWS + j + ROWS] = hnew[1 - par, j]
-        t, blk = where_is(i - 4)
+    def settle_slope(i, par):
+        t, blk = where_is(i)
         for j in range(ROWS):
             s2p[t, blk * ROWS + j + ROWS] = snew[par, j]
 
-    def kernel_grad(i, par):
+    def slopes_of(par):
+        middle = jnp.concatenate([snew[par, j] for j in range(ROWS)], axis=1)
+        return jnp.concatenate([lbuf[par, 0:64], middle, lbuf[par, 64:128]], axis=0)
+
+    def kernel_grad(i):
         t, blk = where_is(i)
-        gacc[...] += mm_nt(lbuf[par], all_taps(hp, t, blk, e2))
+        gacc[...] += mm_nt(
+            jnp.concatenate([slopes_of(0), slopes_of(1)], axis=1),
+            jnp.concatenate([all_taps(hp, t, blk, e2), all_taps(hp, t, blk + 1, e2)], axis=1),
+        )
 
     def row_sums(i, par):
         t, blk = where_is(i)
@@ -190,66 +185,116 @@
                 ],
                 axis=0,
             )
-            u = (u + bvar[t, kind]).astype(EW)
+            u = u + bvar[t, kind]
             th = jnp.tanh(u)
-            w = u * th
-            hnew[par, j] = (u + w).astype(BF)
-            d1[t, x] = ((1.0 + th) * ((1.0 + u) - w)).astype(BF)
+            p = 1.0 + th
+            h = u * p
+            hp[t, x + ROWS] = h.astype(BF)
+            d1[t, x] = (p + h * (1.0 - th)).astype(BF)
+            yield
 
     def phase_two(i, par, z):
         t, blk = where_is(i)
         og = ogacc[...]
         for j in range(ROWS):
-            cols = z[:, j * TILE:(j + 1) * TILE]
+            cols = z(j)
             sides = roll16(cols[0:64].astype(BF), 0) + roll16(cols[128:192].astype(BF), 1)
             u = cols[64:128] + sides.astype(F32)
             th = jnp.tanh(u)
-            w = u * th
+            p = 1.0 + th
+            h = u * p
             m = msk[t, pl.ds(blk * ROWS + j, 1), :]
-            og = og + (u + w) * m
-            s = ((outh[...] * m) * ((1.0 + th) * ((1.0 + u) - w))).astype(BF)
+            og = og + h * m
+            s = (m * (p + h * (1.0 - th))).astype(BF)
             snew[par, j] = s
             lbuf[par, 0:64, j * TILE:(j + 1) * TILE] = roll16(s, 1)
-            lbuf[par, 64:128, j * TILE:(j + 1) * TILE] = s
-            lbuf[par, 128:192, j * TILE:(j + 1) * TILE] = roll16(s, 0)
-        ogacc[...] = og
+            lbuf[par, 64:128, j * TILE:(j + 1) * TILE] = roll16(s, 0)
+            if j == ROWS - 1:
+                ogacc[...] = og
+            yield
 
     def phase_three(i, par, z):
         t, blk = where_is(i)
         slot = jnp.where(blk == 0, 0, jnp.where(blk == BLOCKS - 1, 1, 2))
-        slopes = []
+        total = csacc[t]
         for j in range(ROWS):
-            cols = z[:, j * TILE:(j + 1) * TILE]
+            cols = z(j)
             sides = roll16(cols[0:64].astype(BF), 1) + roll16(cols[128:192].astype(BF), 0)
             back = cols[64:128] + sides.astype(F32)
             s = back * d1[t, blk * ROWS + j].astype(F32)
-            slopes.append(s)
+            total = total + s
             s = s.astype(BF)
             edge[t, slot, j] = s
             p, q = j // 2, j % 2
             sbuf[par, CHAN * p:CHAN * p + CHAN, TILE * q:TILE * q + TILE] = s
-        while len(slopes) > 1:
-            slopes = [slopes[k] + slopes[k + 1] for k in range(0, len(slopes), 2)]
-        csacc[t] += slopes[0]
-
-    def step(i, par):
-        settle(i, par)
-        t, blk = where_is(i - 5)
-        z3 = mm(wmat[5], all_taps(s2p, t, blk, -e2))
-        t, blk = where_is(i - 2)
-        z2 = mm(wmat[4], all_taps(hp, t, blk, e2))
-        kernel_grad(i - 4, par)
-        row_sums(i - 7, par)
-        phase_one(i, par)
-        phase_three(i - 5, par, z3)
-        phase_two(i - 2, par, z2)
+            if j == ROWS - 1:
+                csacc[t] = total
+            yield
+
+    def run(*phases):
+        phases = list(phases)
+        while phases:
+            for phase in list(phases):
+                try:
+                    next(phase)
+                except StopIteration:
+                    phases.remove(phase)
+
+    last = n_tiles * BLOCKS
+
+    def has(i, lag):
+        return not isinstance(i, int) or 0 <= i - lag < last
+
+    def back_product(i):
+        if has(i, 5):
+            t, blk = where_is(i - 5)
+            return mm(wmat[5], all_taps(s2p, t, blk, -e2))
+
+    def map_product(i):
+        if has(i, 2):
+            t, blk = where_is(i - 2)
+            return mm(wmat[4], all_taps(hp, t, blk, e2))
+
+    def settle(i, par):
+        if has(i, 4):
+            settle_slope(i - 4, par)
+
+    def sums(i, par):
+        if par == 0 and has(i, 4):
+            kernel_grad(i - 4)
+        if has(i, 7):
+            row_sums(i - 7, par)
+
+    def first(i, par):
+        return [phase_one(i, par)] if has(i, 0) else []
+
+    def third(i, par, z):
+        return [phase_three(i - 5, par, z)] if has(i, 5) else []
+
+    def second(i, par, z):
+        return [phase_two(i - 2, par, z)] if has(i, 2) else []
+
+    def fresh(z):
+        return lambda j: z[:, j * TILE:(j + 1) * TILE]
+
+    def pair(i):
+        for k, par in ((i, 0), (i + 1, 1)):
+            settle(k, par)
+            z2, z3 = map_product(k), back_product(k)
+            run(*first(k, par))
+            sums(k, par)
+            run(*second(k, par, fresh(z2)))
+            run(*third(k, par, fresh(z3)))
 
     def two_steps(n, carry):
-        step(2 * n, 0)
-        step(2 * n + 1, 1)
+        pair(2 * n)
         return carry
 
-    lax.fori_loop(0, (n_tiles * BLOCKS + 8) // 2, two_steps, 0)
+    for n in range(4):
+        pair(2 * n)
+    lax.fori_loop(4, last // 2, two_steps, 0)
+    for n in range(last // 2, last // 2 + 4):
+        pair(2 * n)
 
     k1a = jnp.zeros((192, 192), F32)
     k1b = jnp.zeros((192, 192), F32)
@@ -293,7 +338,7 @@
                 k1a[64 * b:64 * b + 64, 64 * a:64 * a + 64]
                 + k1b[64 * a:64 * a + 64, 64 * b:64 * b + 64]
             )
-            two = gacc[64 * b:64 * b + 64, 64 * a:64 * a + 64]
+            two = gacc[64 * b:64 * b + 64, 64 * a:64 * a + 64] * outh[:, 0:CHAN]
             pay_out[64 * tap:64 * tap + 64] = jnp.concatenate([one, two], axis=1).astype(BF)
     grads = jnp.concatenate([lg_acc, rg_acc], axis=0)
     pay_out[576:704] = grads[:, 0:TILE].astype(BF)
@@ -322,15 +367,15 @@
         scratch_shapes=[
             pltpu.VMEM((feats.shape[0], 2 * CHAN), F32),
             pltpu.VMEM((6, 192, 192), BF),
-            pltpu.VMEM((n + 1, STRIDE, CHAN, TILE), BF),
-            pltpu.VMEM((n + 1, TILE, CHAN, TILE), BF),
-            pltpu.VMEM((n + 1, STRIDE, CHAN, TILE), BF),
-            pltpu.VMEM((n + 1, TILE, TILE), F32),
-            pltpu.VMEM((n + 1, 3, CHAN, TILE), F32),
-            pltpu.VMEM((n + 1, 4, CHAN, TILE), F32),
-            pltpu.VMEM((n + 1, 4, CHAN, TILE), F32),
-            pltpu.VMEM((n + 1, 3, ROWS, CHAN, TILE), BF),
-            pltpu.VMEM((n + 1, CHAN, TILE), F32),
+            pltpu.VMEM((n, STRIDE, CHAN, TILE), BF),
+            pltpu.VMEM((n, TILE, CHAN, TILE), BF),
+            pltpu.VMEM((n, STRIDE, CHAN, TILE), BF),
+            pltpu.VMEM((n, TILE, TILE), F32),
+            pltpu.VMEM((n, 3, CHAN, TILE), F32),
+            pltpu.VMEM((n, 4, CHAN, TILE), F32),
+            pltpu.VMEM((n, 4, CHAN, TILE), F32),
+            pltpu.VMEM((n, 3, ROWS, CHAN, TILE), BF),
+            pltpu.VMEM((n, CHAN, TILE), F32),
             pltpu.VMEM((192, 192), F32),
             pltpu.VMEM((2 * TILE, TILE), BF),
             pltpu.VMEM((n, 192, TILE), BF),
@@ -339,12 +384,11 @@
             pltpu.VMEM((CHAN, TILE), EW),
             pltpu.VMEM((2, CHAN, TILE), BF),
             pltpu.VMEM((2, ROWS, CHAN, TILE), BF),
-            pltpu.VMEM((2, ROWS, CHAN, TILE), BF),
-            pltpu.VMEM((2, 192, ROWS * TILE), BF),
+            pltpu.VMEM((2, 128, ROWS * TILE), BF),
             pltpu.VMEM((2, ROWS // 2 * CHAN, 2 * TILE), BF),
             pltpu.VMEM((CHAN, TILE), F32),
         ],
-        compiler_params=pltpu.CompilerParams(vmem_limit_bytes=50 * 1024 * 1024),
+        compiler_params=pltpu.CompilerParams(vmem_limit_bytes=32 * MIB),
         name="tile_work",
     )(dilations, band_width, tile_table, feats, wl, wr, k1, k2, outw, cot)
 
@@ -362,7 +406,7 @@
     )
 
 
-def gather_kernel(own_ref, all_ref, send, recv):
+def gather_kernel(own_ref, cot, all_ref, send, recv, here):
     ranges = lax.axis_size("pos")
     members = lax.axis_size("diag")
     pos = lax.axis_index("pos")
@@ -377,7 +421,8 @@
     def place(owner, base):
         return pl.ds(pl.multiple_of(base + owner * rows, 32), rows)
 
-    all_ref[place(diag, 0), :] = own_ref[...]
+    local = pltpu.make_async_copy(own_ref, all_ref.at[place(diag, 0)], here)
+    local.start()
     copies = []
     first = remote(own_ref, all_ref.at[place(diag, half)], send.at[0], recv.at[0], before)
     first.start()
@@ -398,6 +443,7 @@
         )
         copy.start()
         passed.append(copy)
+    local.wait()
     for copy in copies:
         copy.wait_send()
     first.wait()
@@ -405,146 +451,130 @@
         copy.wait()
 
 
-def gather_call(own):
+def gather_call(own, cot):
     vm = pl.BlockSpec(memory_space=pltpu.VMEM)
     members = lax.axis_size("diag")
     return pl.pallas_call(
         gather_kernel,
         out_shape=jax.ShapeDtypeStruct((2 * members * own.shape[0], own.shape[1]), own.dtype),
-        in_specs=[vm],
+        in_specs=[pl.BlockSpec(memory_space=pltpu.HBM), vm],
         out_specs=vm,
         scratch_shapes=[
             pltpu.SemaphoreType.DMA((2 * members,)),
             pltpu.SemaphoreType.DMA((2 * members,)),
+            pltpu.SemaphoreType.DMA,
         ],
-        compiler_params=pltpu.CompilerParams(collective_id=0, has_side_effects=True),
+        compiler_params=pltpu.CompilerParams(
+            collective_id=0, has_side_effects=True, vmem_limit_bytes=4 * MIB
+        ),
         name="gather_bins",
-    )(own)
+    )(own, cot)
+
+
+def ring(axis, pos, diag):
+    core = lax.rem(pos, 2)
+    far = lax.div(pos, 8)
+    mid = lax.rem(lax.div(pos, 2), 4)
+    if axis == 0:
+        return diag, lambda n: (pos, n)
+    if axis == 1:
+        return far, lambda n: ((n * 4 + mid) * 2 + core, diag)
+    return mid, lambda n: ((far * 4 + n) * 2 + core, diag)
 
 
 def reduce_kernel(
     rows_ref, pay_ref,
     rows_out, all_out,
-    row_buf, core_buf, half_sum, near_buf, near_sum, far_buf, far_all, near_own,
-    row_send, row_recv, core_send, core_recv, near_send, near_recv, far_send, far_recv,
-    back_send, back_recv, last_send, last_recv, pass_send, pass_recv,
+    halo_buf, own_rows, row_buf, core_buf, held, slots,
+    halo_send, halo_recv, row_send, row_recv, core_send, core_recv, ring_send, ring_recv, last_send, last_recv,
 ):
     ranges = lax.axis_size("pos")
     members = lax.axis_size("diag")
     pos = lax.axis_index("pos")
     diag = lax.axis_index("diag")
     core = lax.rem(pos, 2)
-    chip = lax.div(pos, 2)
     count = rows_out.shape[0]
     half = members * count
-    after = lax.rem(pos + 1, ranges)
-    across = lax.rem(pos + ranges + 2 * core - 1, ranges)
-    sibling = (2 * chip + 1 - core, diag)
-
-    diag_ids = [lax.rem(diag + k, members) for k in range(1, members)]
-    diag_devs = [(pos, d) for d in diag_ids]
-    far_ids = [lax.rem(chip + k, FAR) for k in range(1, FAR)]
-    far_devs = [(2 * f + core, diag) for f in far_ids]
-    greet(
-        [(2 * chip + 1 - core, d) for d in range(members)]
-        + diag_devs
-        + far_devs
-        + [(across, d) for d in range(members)]
-    )
-
-    def piece(index, size):
-        return pl.ds(pl.multiple_of(index * size, size), size)
+    after = (lax.rem(pos + 1, ranges), diag)
+    across = (lax.rem(pos + ranges + 2 * core - 1, ranges), diag)
+    sibling = (pos + 1 - 2 * core, diag)
+    rings = [ring(axis, pos, diag) for axis in range(3)]
+    peers = [
+        [rings[axis][1](lax.rem(rings[axis][0] + k, 4)) for k in range(1, 4)] for axis in range(3)
+    ]
+    greet([sibling, across] + peers[0] + peers[1] + peers[2])
+
+    def block(owner):
+        return pl.ds(pl.multiple_of(owner * count, 32), count)
+
+    def mine(base):
+        return pl.ds(pl.multiple_of(base, 16), HALF)
 
     core_copy = remote(
-        pay_ref.at[piece(1 - core, HALF)], core_buf, core_send.at[0], core_recv.at[0], sibling
+        pay_ref.at[mine((1 - core) * HALF)], core_buf, core_send.at[0], core_recv.at[0], sibling
     )
     core_copy.start()
     core_copy.wait_recv()
-    half_sum[...] = (pay_ref[piece(core, HALF), :].astype(F32) + core_buf[...].astype(F32)).astype(BF)
-    near_copies = []
-    for k in range(1, members):
-        copy = remote(
-            half_sum.at[piece(diag_ids[k - 1], SHARE)], near_buf.at[k - 1],
-            near_send.at[k - 1], near_recv.at[k - 1], diag_devs[k - 1],
-        )
-        copy.start()
-        near_copies.append(copy)
-    total = half_sum[piece(diag, SHARE), :].astype(F32)
-    for k in range(1, members):
-        near_copies[k - 1].wait_recv()
-        total = total + near_buf[k - 1].astype(F32)
-    near_sum[...] = total
-    far_copies = []
-    for k in range(1, FAR):
-        copy = remote(
-            near_sum.at[piece(far_ids[k - 1], PIECE)], far_buf.at[k - 1],
-            far_send.at[k - 1], far_recv.at[k - 1], far_devs[k - 1],
-        )
-        copy.start()
-        far_copies.append(copy)
+    total = pay_ref[mine(core * HALF), :].astype(F32) + core_buf[...].astype(F32)
+    held[0] = total.astype(BF)
+
+    sent = [core_copy]
     row_copies = []
-    for k in range(1, 2 * members):
-        owner = lax.rem(diag + k, members)
-        base = 0 if k < members else half
-        target = (pos, owner) if k < members else (after, owner)
-        copy = remote(
-            rows_ref.at[pl.ds(pl.multiple_of(base + owner * count, 32), count)], row_buf.at[k - 1],
-            row_send.at[k - 1], row_recv.at[k - 1], target,
-        )
-        copy.start()
-        row_copies.append(copy)
-
-    mine = near_sum[piece(chip, PIECE), :]
-    for k in range(1, FAR):
-        far_copies[k - 1].wait_recv()
-        mine = mine + far_buf[k - 1]
-    far_all[piece(chip, PIECE), :] = mine * (1.0 / ranges)
-    back_copies = []
-    for k in range(1, FAR):
-        copy = remote(
-            far_all.at[piece(chip, PIECE)], far_all.at[piece(chip, PIECE)],
-            back_send.at[k - 1], back_recv.at[k - 1], far_devs[k - 1],
-        )
-        copy.start()
-        back_copies.append(copy)
-
-    rows = rows_ref[pl.ds(pl.multiple_of(diag * count, 32), count), :].astype(F32)
-    for k in range(1, 2 * members):
-        row_copies[k - 1].wait_recv()
-        rows = rows + row_buf[k - 1].astype(F32)
-    rows_out[...] = rows.astype(BF)
-
-    for k in range(1, FAR):
-        back_copies[k - 1].wait_recv()
-    near_own[...] = far_all[...].astype(BF)
-
-    def spot(owner):
-        return pl.ds(pl.multiple_of(core * HALF + owner * SHARE, SHARE), SHARE)
-
-    last_copies = []
-    for k in range(1, members):
-        copy = remote(
-            near_own, all_out.at[spot(diag)],
-            last_send.at[k - 1], last_recv.at[k - 1], diag_devs[k - 1],
-        )
-        copy.start()
-        last_copies.append(copy)
-    pass_copies = [
-        remote(near_own, all_out.at[spot(diag)], pass_send.at[0], pass_recv.at[0], sibling)
-    ]
-    pass_copies[0].start()
-    all_out[spot(diag), :] = near_own[...]
-    for k in (1, 3, 2):
-        last_copies[k - 1].wait_recv()
-        owner = lax.rem(diag + members - k, members)
-        copy = remote(
-            all_out.at[spot(owner)], all_out.at[spot(owner)], pass_send.at[k], pass_recv.at[k], sibling
-        )
-        copy.start()
-        pass_copies.append(copy)
-    for copy in pass_copies:
-        copy.wait_recv()
-    for copy in [core_copy] + near_copies + row_copies + far_copies + back_copies + last_copies + pass_copies:
+    for phase in range(3):
+        copies = []
+        for part in range(3):
+            axis = (part + phase) % 3
+            place = rings[axis][0]
+            rows = pl.ds(part * THIRD, THIRD)
+            for k in range(1, 4):
+                copy = remote(
+                    held.at[phase, rows], slots.at[phase, part, place],
+                    ring_send.at[phase, part, k - 1], ring_recv.at[phase, part, k - 1],
+                    peers[axis][k - 1],
+                )
+                copy.start()
+                copies.append(copy)
+            slots[phase, part, place] = held[phase, rows, :]
+        sent.extend(copies)
+        if phase == 0:
+            halo_copy = remote(
+                rows_ref.at[pl.ds(half, half)], halo_buf, halo_send.at[0], halo_recv.at[0], after
+            )
+            halo_copy.start()
+            sent.append(halo_copy)
+        if phase == 1:
+            halo_copy.wait_recv()
+            own_rows[...] = (rows_ref[0:half, :].astype(F32) + halo_buf[...].astype(F32)).astype(BF)
+            for k in range(1, members):
+                copy = remote(
+                    own_rows.at[block(lax.rem(diag + k, members))], row_buf.at[k - 1],
+                    row_send.at[k - 1], row_recv.at[k - 1], peers[0][k - 1],
+                )
+                copy.start()
+                row_copies.append(copy)
+        if phase == 2:
+            rows = own_rows[block(diag), :].astype(F32)
+            for k in range(1, members):
+                row_copies[k - 1].wait_recv()
+                rows = rows + row_buf[k - 1].astype(F32)
+            rows_out[...] = rows.astype(BF)
+        for part in range(3):
+            for k in range(3):
+                copies[3 * part + k].wait_recv()
+            total = slots[phase, part, 0].astype(F32)
+            for place in range(1, 4):
+                total = total + slots[phase, part, place].astype(F32)
+            if phase == 2:
+                total = total * (1.0 / ranges)
+            held[phase + 1, pl.ds(part * THIRD, THIRD), :] = total.astype(BF)
+
+    last_copy = remote(
+        held.at[3], all_out.at[mine(core * HALF)], last_send.at[0], last_recv.at[0], sibling
+    )
+    last_copy.start()
+    all_out[mine(core * HALF), :] = held[3]
+    last_copy.wait_recv()
+    for copy in sent + row_copies + [last_copy]:
         copy.wait_send()
 
 
@@ -562,23 +592,21 @@
         in_specs=[vm] * 2,
         out_specs=(vm,) * 2,
         scratch_shapes=[
-            pltpu.VMEM((2 * members - 1, count, 2 * CHAN), BF),
+            pltpu.VMEM((members * count, 2 * CHAN), BF),
+            pltpu.VMEM((members * count, 2 * CHAN), BF),
+            pltpu.VMEM((members - 1, count, 2 * CHAN), BF),
             pltpu.VMEM((HALF, TILE), BF),
-            pltpu.VMEM((HALF, TILE), BF),
-            pltpu.VMEM((members - 1, SHARE, TILE), BF),
-            pltpu.VMEM((SHARE, TILE), F32),
-            pltpu.VMEM((FAR - 1, PIECE, TILE), F32),
-            pltpu.VMEM((SHARE, TILE), F32),
-            pltpu.VMEM((SHARE, TILE), BF),
-            dma((2 * members - 1,)), dma((2 * members - 1,)),
+            pltpu.VMEM((4, HALF, TILE), BF),
+            pltpu.VMEM((3, 3, 4, THIRD, TILE), BF),
             dma((1,)), dma((1,)),
             dma((members - 1,)), dma((members - 1,)),
-            dma((FAR - 1,)), dma((FAR - 1,)),
-            dma((FAR - 1,)), dma((FAR - 1,)),
-            dma((members - 1,)), dma((members - 1,)),
-            dma((members,)), dma((members,)),
+            dma((1,)), dma((1,)),
+            dma((3, 3, 3)), dma((3, 3, 3)),
+            dma((1,)), dma((1,)),
         ],
-        compiler_params=pltpu.CompilerParams(collective_id=1, has_side_effects=True),
+        compiler_params=pltpu.CompilerParams(
+            collective_id=1, has_side_effects=True, vmem_limit_bytes=6 * MIB
+        ),
         name="reduce_grads",
     )(rows, payload)
 
@@ -611,6 +639,7 @@
         ),
         in_specs=[vm] * 4,
         out_specs=(vm,) * 5,
+        compiler_params=pltpu.CompilerParams(vmem_limit_bytes=6 * MIB),
         name="finish",
     )(rows, sums, wl, wr)
 
@@ -629,7 +658,7 @@
 ):
     left_t = left_weight.T
     right_t = right_weight.T
-    feats = gather_call(bin_features)
+    feats = gather_call(bin_features, cotangent)
     rows, payload = tile_call(
         dilations, band_width, tile_table, feats, left_t, right_t,
         kernel_one, kernel_two, out_weight.reshape(1, CHAN), cotangent,

time: 87 us -> 69 us (0.79)
  Pallas kernels: 82.1 us -> 65.7 us
  local copies, waits for them, and re-layouts: 3.29 us -> 1.72 us
    pallas_call x1, Pallas kernels: 29.5 us -> 22.3 us  [reduce_call(): pl.pallas_call(reduce_kernel, out_shape=(jax.ShapeDtypeStruct((count, 2 *...]
    pallas_call x1, Pallas kernels: 36 us -> 29.2 us  [tile_call(): pl.pallas_call(tile_kernel, out_shape=(jax.ShapeDtypeStruct((feats.shape[...]
    unnamed x22 -> x20, local copies, waits for them, and re-layouts: 3.29 us -> 1.72 us
    pallas_call x1, Pallas kernels: 14.7 us -> 13.1 us  [gather_call(): pl.pallas_call(gather_kernel, out_shape=jax.ShapeDtypeStruct((2 * members...]
    pallas_call x1, Pallas kernels: 1.93 us -> 0.97 us  [finish_call(): pl.pallas_call(finish_kernel, out_shape=(jax.ShapeDtypeStruct((rows.shape...]
where the time goes in v3:
time: 69 us; the launch traced here: 68.8 us
  Pallas kernels  65.7 us (95%)
  local copies, waits for them, and re-layouts  1.72 us (2%)
  between operations  1.41 us (2%)
    pallas_call x1, Pallas kernels, tile_call(): pl.pallas_call(tile_kernel, out_shape=(jax.ShapeDtypeStruct((feats.shape[...  29.2 us
    pallas_call x1, Pallas kernels, reduce_call(): pl.pallas_call(reduce_kernel, out_shape=(jax.ShapeDtypeStruct((count, 2 *...  22.3 us
    pallas_call x1, Pallas kernels, gather_call(): pl.pallas_call(gather_kernel, out_shape=jax.ShapeDtypeStruct((2 * members...  13.1 us
    unnamed x20, local copies, waits for them, and re-layouts  1.72 us

profile of v3, /device:TPU:1, one launch (start us, length us, event | category | flops | bytes accessed | tf_op | source)
XLA Modules:
  0.0 68.8 jit_solution(8114126436096415737)
XLA Ops:
  1.3 0.0 copy-start
  1.3 0.9 %copy-done = bf16[3,128,128]{2,1,0:T(8,128)(2,1)S(1)} copy-done((bf16[3,128,128]{2,1,0:T(8,128)(2,1)S(1)}, bf16[3,128,128]{2,1,0:T(8,128)(2,1)}, u32[]{:S(2)}) %copy-start) | copy-done | bytes 98328
  2.2 0.0 copy-start.6
  2.2 0.8 %copy-done.6 = bf16[96,256]{1,0:T(8,128)(2,1)S(1)} copy-done((bf16[96,256]{1,0:T(8,128)(2,1)S(1)}, bf16[96,256]{1,0:T(8,128)(2,1)}, u32[]{:S(2)}) %copy-start.6) | copy-done | bytes 49176
  3.0 0.0 copy-start.1
  3.0 0.0 copy-start.2
  3.0 0.0 copy-start.3
  3.0 0.0 copy-start.4
  3.0 0.0 copy-start.5
  3.0 0.0 copy-start.7
  3.0 0.0 copy-start.8
  3.0 0.0 copy-start.9
  3.0 13.1 %gather_bins.1.feats = bf16[768,256]{1,0:T(8,128)(2,1)S(1)} custom-call(bf16[96,256]{1,0:T(8,128)(2,1)S(1)} %copy-done.6, bf16[3,128,128]{2,1,0:T(8,128)(2,1)S(1)} %copy-done), custom_call_target="tpu_custom_call" | custom-call | tf_op jit(solution)/shard_map/gather_bins/pallas_call | solution.py:457
  16.2 0.0 copy-done.1
  16.2 0.0 copy-done.2
  16.2 0.0 copy-done.3
  16.2 0.0 copy-done.4
  16.2 0.0 copy-done.5
  16.2 0.0 copy-done.7
  16.2 0.0 copy-done.8
  16.2 0.0 copy-done.9
  16.2 29.2 %tile_work.1 = (bf16[768,128]{1,0:T(8,128)(2,1)S(1)}, bf16[864,128]{1,0:T(8,128)(2,1)S(1)}) custom-call(s32[2]{0:T(128)S(1)} %copy-done.7, s32[1]{0:T(128)S(6)} %copy.15.bandw, s32[1,12]{1,0:T(1,128)S(1)} %copy-done.8, bf16[768,256]{1,0:T(8,128)(2,1)S(1)} %gather_bins.1.feats, bf16[64,256]{1,0:T(8,128)(2,1)S(1)} %bitcast.6, bf16[64,256]{1,0:T(8,128)(2,1)S(1)} %bitcast.8, ...), custom_call_target="tpu_custom_call" | custom-call | tf_op jit(solution)/shard_map/tile_work/pallas_call | solution.py:359
  45.5 22.3 %reduce_grads.1 = (bf16[96,128]{1,0:T(8,128)(2,1)S(1)}, bf16[864,128]{1,0:T(8,128)(2,1)S(1)}) custom-call(bf16[768,128]{1,0:T(8,128)(2,1)S(1)} %get-tuple-element.14.rows_ref, bf16[864,128]{1,0:T(8,128)(2,1)S(1)} %get-tuple-element.15.pay_ref), custom_call_target="tpu_custom_call" | custom-call | tf_op jit(solution)/shard_map/reduce_grads/pallas_call | solution.py:586
  67.8 1.0 %finish.1 = (f32[96,256]{1,0:T(8,128)}, f32[64,256]{1,0:T(8,128)}, f32[64,256]{1,0:T(8,128)}, f32[2,9,64,64]{3,2,1,0:T(8,128)}, f32[1,64]{1,0:T(1,128)}) custom-call(bf16[96,128]{1,0:T(8,128)(2,1)S(1)} %get-tuple-element.16.rows, bf16[864,128]{1,0:T(8,128)(2,1)S(1)} %get-tuple-element.17.sums, bf16[64,256]{1,0:T(8,128)(2,1)S(1)} %bitcast.7, ...), custom_call_target="tpu_custom_call" | custom-call | tf_op jit(solution)/shard_map/finish/pallas_call | solution.py:631
Async XLA Ops:
  1.3 0.9 %copy-start = (bf16[3,128,128]{2,1,0:T(8,128)(2,1)S(1)}, bf16[3,128,128]{2,1,0:T(8,128)(2,1)}, u32[]{:S(2)}) copy-start(bf16[3,128,128]{2,1,0:T(8,128)(2,1)} %cot.3) | copy-start | bytes 294916
  2.2 0.8 %copy-start.6 = (bf16[96,256]{1,0:T(8,128)(2,1)S(1)}, bf16[96,256]{1,0:T(8,128)(2,1)}, u32[]{:S(2)}) copy-start(bf16[96,256]{1,0:T(8,128)(2,1)} %own_ref.1) | copy-start | bytes 147460
  3.0 13.2 %copy-start.1 = (bf16[3,128,128]{2,1,0:T(8,128)(2,1)S(1)}, bf16[3,128,128]{2,1,0:T(8,128)(2,1)}, u32[]{:S(2)}) copy-start(bf16[3,128,128]{2,1,0:T(8,128)(2,1)} %cot.3) | copy-start | bytes 294916
  3.0 13.2 %copy-start.2 = (bf16[9,64,64]{2,1,0:T(8,128)(2,1)S(1)}, bf16[9,64,64]{2,1,0:T(8,128)(2,1)}, u32[]{:S(2)}) copy-start(bf16[9,64,64]{2,1,0:T(8,128)(2,1)} %k1.1) | copy-start | bytes 221188
  3.0 13.2 %copy-start.3 = (bf16[9,64,64]{2,1,0:T(8,128)(2,1)S(1)}, bf16[9,64,64]{2,1,0:T(8,128)(2,1)}, u32[]{:S(2)}) copy-start(bf16[9,64,64]{2,1,0:T(8,128)(2,1)} %k2.1) | copy-start | bytes 221188
  3.0 13.2 %copy-start.4 = (bf16[256,64]{0,1:T(8,128)(2,1)S(1)}, bf16[256,64]{0,1:T(8,128)(2,1)}, u32[]{:S(2)}) copy-start(bf16[256,64]{0,1:T(8,128)(2,1)} %param.11) | copy-start | bytes 98308
  3.0 13.2 %copy-start.5 = (bf16[256,64]{0,1:T(8,128)(2,1)S(1)}, bf16[256,64]{0,1:T(8,128)(2,1)}, u32[]{:S(2)}) copy-start(bf16[256,64]{0,1:T(8,128)(2,1)} %param.12) | copy-start | bytes 98308
  3.0 13.2 %copy-start.7 = (s32[2]{0:T(128)S(1)}, s32[2]{0:T(128)}, u32[]{:S(2)}) copy-start(s32[2]{0:T(128)} %dil.1) | copy-start | bytes 28
  3.0 13.2 %copy-start.8 = (s32[1,12]{1,0:T(1,128)S(1)}, s32[1,12]{1,0:T(1,128)}, u32[]{:S(2)}) copy-start(s32[1,12]{1,0:T(1,128)} %table.1) | copy-start | bytes 148
  3.0 13.2 %copy-start.9 = (bf16[64]{0:T(256)(128)(2,1)S(1)}, bf16[64]{0:T(256)(128)(2,1)}, u32[]{:S(2)}) copy-start(bf16[64]{0:T(256)(128)(2,1)} %param.15) | copy-start | bytes 388

commit v4 on v3

--- a/solution.py
+++ b/solution.py
@@ -185,7 +185,7 @@
                 ],
                 axis=0,
             )
-            u = u + bvar[t, kind]
+            u = (u + bvar[t, kind]).astype(BF)
             th = jnp.tanh(u)
             p = 1.0 + th
             h = u * p
@@ -199,13 +199,13 @@
         for j in range(ROWS):
             cols = z(j)
             sides = roll16(cols[0:64].astype(BF), 0) + roll16(cols[128:192].astype(BF), 1)
-            u = cols[64:128] + sides.astype(F32)
+            u = cols[64:128].astype(BF) + sides
             th = jnp.tanh(u)
             p = 1.0 + th
             h = u * p
             m = msk[t, pl.ds(blk * ROWS + j, 1), :]
-            og = og + h * m
-            s = (m * (p + h * (1.0 - th))).astype(BF)
+            og = og + h.astype(F32) * m
+            s = m.astype(BF) * (p + h * (1.0 - th))
             snew[par, j] = s
             lbuf[par, 0:64, j * TILE:(j + 1) * TILE] = roll16(s, 1)
             lbuf[par, 64:128, j * TILE:(j + 1) * TILE] = roll16(s, 0)
@@ -220,10 +220,9 @@
         for j in range(ROWS):
             cols = z(j)
             sides = roll16(cols[0:64].astype(BF), 1) + roll16(cols[128:192].astype(BF), 0)
-            back = cols[64:128] + sides.astype(F32)
-            s = back * d1[t, blk * ROWS + j].astype(F32)
-            total = total + s
-            s = s.astype(BF)
+            back = cols[64:128].astype(BF) + sides
+            s = back * d1[t, blk * ROWS + j]
+            total = total + s.astype(F32)
             edge[t, slot, j] = s
             p, q = j // 2, j % 2
             sbuf[par, CHAN * p:CHAN * p + CHAN, TILE * q:TILE * q + TILE] = s

time: 69 us -> 67.2 us (0.974)
  Pallas kernels: 65.7 us -> 63.9 us
    pallas_call x1, Pallas kernels: 29.2 us -> 27.4 us  [tile_call(): pl.pallas_call(tile_kernel, out_shape=(jax.ShapeDtypeStruct((feats.shape[...]
where the time goes in v4:
time: 67.2 us; the launch traced here: 67 us
  Pallas kernels  63.9 us (95%)
  local copies, waits for them, and re-layouts  1.72 us (3%)
  between operations  1.41 us (2%)
    pallas_call x1, Pallas kernels, tile_call(): pl.pallas_call(tile_kernel, out_shape=(jax.ShapeDtypeStruct((feats.shape[...  27.4 us
    pallas_call x1, Pallas kernels, reduce_call(): pl.pallas_call(reduce_kernel, out_shape=(jax.ShapeDtypeStruct((count, 2 *...  22.3 us
    pallas_call x1, Pallas kernels, gather_call(): pl.pallas_call(gather_kernel, out_shape=jax.ShapeDtypeStruct((2 * members...  13.1 us
    unnamed x20, local copies, waits for them, and re-layouts  1.72 us

profile of v4, /device:TPU:1, one launch (start us, length us, event | category | flops | bytes accessed | tf_op | source)
XLA Modules:
  0.0 67.0 jit_solution(8770055408331234936)
XLA Ops:
  1.3 0.0 copy-start
  1.3 0.9 %copy-done = bf16[3,128,128]{2,1,0:T(8,128)(2,1)S(1)} copy-done((bf16[3,128,128]{2,1,0:T(8,128)(2,1)S(1)}, bf16[3,128,128]{2,1,0:T(8,128)(2,1)}, u32[]{:S(2)}) %copy-start) | copy-done | bytes 98328
  2.2 0.0 copy-start.6
  2.2 0.8 %copy-done.6 = bf16[96,256]{1,0:T(8,128)(2,1)S(1)} copy-done((bf16[96,256]{1,0:T(8,128)(2,1)S(1)}, bf16[96,256]{1,0:T(8,128)(2,1)}, u32[]{:S(2)}) %copy-start.6) | copy-done | bytes 49176
  3.0 0.0 copy-start.1
  3.0 0.0 copy-start.2
  3.0 0.0 copy-start.3
  3.0 0.0 copy-start.4
  3.0 0.0 copy-start.5
  3.0 0.0 copy-start.7
  3.0 0.0 copy-start.8
  3.0 0.0 copy-start.9
  3.0 13.1 %gather_bins.1.feats = bf16[768,256]{1,0:T(8,128)(2,1)S(1)} custom-call(bf16[96,256]{1,0:T(8,128)(2,1)S(1)} %copy-done.6, bf16[3,128,128]{2,1,0:T(8,128)(2,1)S(1)} %copy-done), custom_call_target="tpu_custom_call" | custom-call | tf_op jit(solution)/shard_map/gather_bins/pallas_call | solution.py:456
  16.2 0.0 copy-done.1
  16.2 0.0 copy-done.2
  16.2 0.0 copy-done.3
  16.2 0.0 copy-done.4
  16.2 0.0 copy-done.5
  16.2 0.0 copy-done.7
  16.2 0.0 copy-done.8
  16.2 0.0 copy-done.9
  16.2 27.4 %tile_work.1 = (bf16[768,128]{1,0:T(8,128)(2,1)S(1)}, bf16[864,128]{1,0:T(8,128)(2,1)S(1)}) custom-call(s32[2]{0:T(128)S(1)} %copy-done.7, s32[1]{0:T(128)S(6)} %copy.15.bandw, s32[1,12]{1,0:T(1,128)S(1)} %copy-done.8, bf16[768,256]{1,0:T(8,128)(2,1)S(1)} %gather_bins.1.feats, bf16[64,256]{1,0:T(8,128)(2,1)S(1)} %bitcast.6, bf16[64,256]{1,0:T(8,128)(2,1)S(1)} %bitcast.8, ...), custom_call_target="tpu_custom_call" | custom-call | tf_op jit(solution)/shard_map/tile_work/pallas_call | solution.py:358
  43.7 22.3 %reduce_grads.1 = (bf16[96,128]{1,0:T(8,128)(2,1)S(1)}, bf16[864,128]{1,0:T(8,128)(2,1)S(1)}) custom-call(bf16[768,128]{1,0:T(8,128)(2,1)S(1)} %get-tuple-element.14.rows_ref, bf16[864,128]{1,0:T(8,128)(2,1)S(1)} %get-tuple-element.15.pay_ref), custom_call_target="tpu_custom_call" | custom-call | tf_op jit(solution)/shard_map/reduce_grads/pallas_call | solution.py:585
  66.0 1.0 %finish.1 = (f32[96,256]{1,0:T(8,128)}, f32[64,256]{1,0:T(8,128)}, f32[64,256]{1,0:T(8,128)}, f32[2,9,64,64]{3,2,1,0:T(8,128)}, f32[1,64]{1,0:T(1,128)}) custom-call(bf16[96,128]{1,0:T(8,128)(2,1)S(1)} %get-tuple-element.16.rows, bf16[864,128]{1,0:T(8,128)(2,1)S(1)} %get-tuple-element.17.sums, bf16[64,256]{1,0:T(8,128)(2,1)S(1)} %bitcast.7, ...), custom_call_target="tpu_custom_call" | custom-call | tf_op jit(solution)/shard_map/finish/pallas_call | solution.py:630
Async XLA Ops:
  1.3 0.9 %copy-start = (bf16[3,128,128]{2,1,0:T(8,128)(2,1)S(1)}, bf16[3,128,128]{2,1,0:T(8,128)(2,1)}, u32[]{:S(2)}) copy-start(bf16[3,128,128]{2,1,0:T(8,128)(2,1)} %cot.3) | copy-start | bytes 294916
  2.2 0.8 %copy-start.6 = (bf16[96,256]{1,0:T(8,128)(2,1)S(1)}, bf16[96,256]{1,0:T(8,128)(2,1)}, u32[]{:S(2)}) copy-start(bf16[96,256]{1,0:T(8,128)(2,1)} %own_ref.1) | copy-start | bytes 147460
  3.0 13.2 %copy-start.1 = (bf16[3,128,128]{2,1,0:T(8,128)(2,1)S(1)}, bf16[3,128,128]{2,1,0:T(8,128)(2,1)}, u32[]{:S(2)}) copy-start(bf16[3,128,128]{2,1,0:T(8,128)(2,1)} %cot.3) | copy-start | bytes 294916
  3.0 13.2 %copy-start.2 = (bf16[9,64,64]{2,1,0:T(8,128)(2,1)S(1)}, bf16[9,64,64]{2,1,0:T(8,128)(2,1)}, u32[]{:S(2)}) copy-start(bf16[9,64,64]{2,1,0:T(8,128)(2,1)} %k1.1) | copy-start | bytes 221188
  3.0 13.2 %copy-start.3 = (bf16[9,64,64]{2,1,0:T(8,128)(2,1)S(1)}, bf16[9,64,64]{2,1,0:T(8,128)(2,1)}, u32[]{:S(2)}) copy-start(bf16[9,64,64]{2,1,0:T(8,128)(2,1)} %k2.1) | copy-start | bytes 221188
  3.0 13.2 %copy-start.4 = (bf16[256,64]{0,1:T(8,128)(2,1)S(1)}, bf16[256,64]{0,1:T(8,128)(2,1)}, u32[]{:S(2)}) copy-start(bf16[256,64]{0,1:T(8,128)(2,1)} %param.11) | copy-start | bytes 98308
  3.0 13.2 %copy-start.5 = (bf16[256,64]{0,1:T(8,128)(2,1)S(1)}, bf16[256,64]{0,1:T(8,128)(2,1)}, u32[]{:S(2)}) copy-start(bf16[256,64]{0,1:T(8,128)(2,1)} %param.12) | copy-start | bytes 98308
  3.0 13.2 %copy-start.7 = (s32[2]{0:T(128)S(1)}, s32[2]{0:T(128)}, u32[]{:S(2)}) copy-start(s32[2]{0:T(128)} %dil.1) | copy-start | bytes 28
  3.0 13.2 %copy-start.8 = (s32[1,12]{1,0:T(1,128)S(1)}, s32[1,12]{1,0:T(1,128)}, u32[]{:S(2)}) copy-start(s32[1,12]{1,0:T(1,128)} %table.1) | copy-start | bytes 148
  3.0 13.2 %copy-start.9 = (bf16[64]{0:T(256)(128)(2,1)S(1)}, bf16[64]{0:T(256)(128)(2,1)}, u32[]{:S(2)}) copy-start(bf16[64]{0:T(256)(128)(2,1)} %param.15) | copy-start | bytes 388

commit v5 on v4

--- a/solution.py
+++ b/solution.py
@@ -506,18 +506,20 @@
     def block(owner):
         return pl.ds(pl.multiple_of(owner * count, 32), count)
 
-    def mine(base):
-        return pl.ds(pl.multiple_of(base, 16), HALF)
-
-    core_copy = remote(
-        pay_ref.at[mine((1 - core) * HALF)], core_buf, core_send.at[0], core_recv.at[0], sibling
-    )
-    core_copy.start()
-    core_copy.wait_recv()
-    total = pay_ref[mine(core * HALF), :].astype(F32) + core_buf[...].astype(F32)
-    held[0] = total.astype(BF)
-
-    sent = [core_copy]
+    def third(base, part):
+        return pl.ds(pl.multiple_of(base + part * THIRD, 16), THIRD)
+
+    core_copies = []
+    for part in range(3):
+        copy = remote(
+            pay_ref.at[third((1 - core) * HALF, part)], core_buf.at[third(0, part)],
+            core_send.at[part], core_recv.at[part], sibling,
+        )
+        copy.start()
+        core_copies.append(copy)
+
+    sent = list(core_copies)
+    last_copies = []
     row_copies = []
     for phase in range(3):
         copies = []
@@ -525,7 +527,11 @@
             axis = (part + phase) % 3
             place = rings[axis][0]
             rows = pl.ds(part * THIRD, THIRD)
-            for k in range(1, 4):
+            if phase == 0:
+                core_copies[part].wait_recv()
+                total = pay_ref[third(core * HALF, part), :].astype(F32) + core_buf[rows, :].astype(F32)
+                held[0, rows, :] = total.astype(BF)
+            for k in (2, 1, 3):
                 copy = remote(
                     held.at[phase, rows], slots.at[phase, part, place],
                     ring_send.at[phase, part, k - 1], ring_recv.at[phase, part, k - 1],
@@ -563,17 +569,22 @@
             total = slots[phase, part, 0].astype(F32)
             for place in range(1, 4):
                 total = total + slots[phase, part, place].astype(F32)
-            if phase == 2:
-                total = total * (1.0 / ranges)
-            held[phase + 1, pl.ds(part * THIRD, THIRD), :] = total.astype(BF)
-
-    last_copy = remote(
-        held.at[3], all_out.at[mine(core * HALF)], last_send.at[0], last_recv.at[0], sibling
-    )
-    last_copy.start()
-    all_out[mine(core * HALF), :] = held[3]
-    last_copy.wait_recv()
-    for copy in sent + row_copies + [last_copy]:
+            rows = pl.ds(part * THIRD, THIRD)
+            if phase < 2:
+                held[phase + 1, rows, :] = total.astype(BF)
+                continue
+            held[3, rows, :] = (total * (1.0 / ranges)).astype(BF)
+            copy = remote(
+                held.at[3, rows], all_out.at[third(core * HALF, part)],
+                last_send.at[part], last_recv.at[part], sibling,
+            )
+            copy.start()
+            last_copies.append(copy)
+            all_out[third(core * HALF, part), :] = held[3, rows, :]
+
+    for copy in last_copies:
+        copy.wait_recv()
+    for copy in sent + row_copies + last_copies:
         copy.wait_send()
 
 
@@ -599,9 +610,9 @@
             pltpu.VMEM((3, 3, 4, THIRD, TILE), BF),
             dma((1,)), dma((1,)),
             dma((members - 1,)), dma((members - 1,)),
-            dma((1,)), dma((1,)),
+            dma((3,)), dma((3,)),
             dma((3, 3, 3)), dma((3, 3, 3)),
-            dma((1,)), dma((1,)),
+            dma((3,)), dma((3,)),
         ],
         compiler_params=pltpu.CompilerParams(
             collective_id=1, has_side_effects=True, vmem_limit_bytes=6 * MIB

time: 67.2 us -> 66.4 us (0.988)
  Pallas kernels: 63.9 us -> 63.1 us
    pallas_call x1, Pallas kernels: 22.3 us -> 21.5 us  [reduce_call(): pl.pallas_call(reduce_kernel, out_shape=(jax.ShapeDtypeStruct((count, 2 *...]
where the time goes in v5:
time: 66.4 us; the launch traced here: 66.2 us
  Pallas kernels  63.1 us (95%)
  local copies, waits for them, and re-layouts  1.72 us (3%)
  between operations  1.41 us (2%)
    pallas_call x1, Pallas kernels, tile_call(): pl.pallas_call(tile_kernel, out_shape=(jax.ShapeDtypeStruct((feats.shape[...  27.4 us
    pallas_call x1, Pallas kernels, reduce_call(): pl.pallas_call(reduce_kernel, out_shape=(jax.ShapeDtypeStruct((count, 2 *...  21.5 us
    pallas_call x1, Pallas kernels, gather_call(): pl.pallas_call(gather_kernel, out_shape=jax.ShapeDtypeStruct((2 * members...  13.1 us
    unnamed x20, local copies, waits for them, and re-layouts  1.72 us

profile of v5, /device:TPU:1, one launch (start us, length us, event | category | flops | bytes accessed | tf_op | source)
XLA Modules:
  0.0 66.2 jit_solution(18432413323662186006)
XLA Ops:
  1.3 0.0 copy-start
  1.3 0.9 %copy-done = bf16[3,128,128]{2,1,0:T(8,128)(2,1)S(1)} copy-done((bf16[3,128,128]{2,1,0:T(8,128)(2,1)S(1)}, bf16[3,128,128]{2,1,0:T(8,128)(2,1)}, u32[]{:S(2)}) %copy-start) | copy-done | bytes 98328
  2.2 0.0 copy-start.6
  2.2 0.8 %copy-done.6 = bf16[96,256]{1,0:T(8,128)(2,1)S(1)} copy-done((bf16[96,256]{1,0:T(8,128)(2,1)S(1)}, bf16[96,256]{1,0:T(8,128)(2,1)}, u32[]{:S(2)}) %copy-start.6) | copy-done | bytes 49176
  3.0 0.0 copy-start.1
  3.0 0.0 copy-start.2
  3.0 0.0 copy-start.3
  3.0 0.0 copy-start.4
  3.0 0.0 copy-start.5
  3.0 0.0 copy-start.7
  3.0 0.0 copy-start.8
  3.0 0.0 copy-start.9
  3.0 13.1 %gather_bins.1.feats = bf16[768,256]{1,0:T(8,128)(2,1)S(1)} custom-call(bf16[96,256]{1,0:T(8,128)(2,1)S(1)} %copy-done.6, bf16[3,128,128]{2,1,0:T(8,128)(2,1)S(1)} %copy-done), custom_call_target="tpu_custom_call" | custom-call | tf_op jit(solution)/shard_map/gather_bins/pallas_call | solution.py:456
  16.2 0.0 copy-done.1
  16.2 0.0 copy-done.2
  16.2 0.0 copy-done.3
  16.2 0.0 copy-done.4
  16.2 0.0 copy-done.5
  16.2 0.0 copy-done.7
  16.2 0.0 copy-done.8
  16.2 0.0 copy-done.9
  16.2 27.4 %tile_work.1 = (bf16[768,128]{1,0:T(8,128)(2,1)S(1)}, bf16[864,128]{1,0:T(8,128)(2,1)S(1)}) custom-call(s32[2]{0:T(128)S(1)} %copy-done.7, s32[1]{0:T(128)S(6)} %copy.15.bandw, s32[1,12]{1,0:T(1,128)S(1)} %copy-done.8, bf16[768,256]{1,0:T(8,128)(2,1)S(1)} %gather_bins.1.feats, bf16[64,256]{1,0:T(8,128)(2,1)S(1)} %bitcast.6, bf16[64,256]{1,0:T(8,128)(2,1)S(1)} %bitcast.8, ...), custom_call_target="tpu_custom_call" | custom-call | tf_op jit(solution)/shard_map/tile_work/pallas_call | solution.py:358
  43.7 21.5 %reduce_grads.1 = (bf16[96,128]{1,0:T(8,128)(2,1)S(1)}, bf16[864,128]{1,0:T(8,128)(2,1)S(1)}) custom-call(bf16[768,128]{1,0:T(8,128)(2,1)S(1)} %get-tuple-element.14.rows_ref, bf16[864,128]{1,0:T(8,128)(2,1)S(1)} %get-tuple-element.15.pay_ref), custom_call_target="tpu_custom_call" | custom-call | tf_op jit(solution)/shard_map/reduce_grads/pallas_call | solution.py:596
  65.2 1.0 %finish.1 = (f32[96,256]{1,0:T(8,128)}, f32[64,256]{1,0:T(8,128)}, f32[64,256]{1,0:T(8,128)}, f32[2,9,64,64]{3,2,1,0:T(8,128)}, f32[1,64]{1,0:T(1,128)}) custom-call(bf16[96,128]{1,0:T(8,128)(2,1)S(1)} %get-tuple-element.16.rows, bf16[864,128]{1,0:T(8,128)(2,1)S(1)} %get-tuple-element.17.sums, bf16[64,256]{1,0:T(8,128)(2,1)S(1)} %bitcast.7, ...), custom_call_target="tpu_custom_call" | custom-call | tf_op jit(solution)/shard_map/finish/pallas_call | solution.py:641
Async XLA Ops:
  1.3 0.9 %copy-start = (bf16[3,128,128]{2,1,0:T(8,128)(2,1)S(1)}, bf16[3,128,128]{2,1,0:T(8,128)(2,1)}, u32[]{:S(2)}) copy-start(bf16[3,128,128]{2,1,0:T(8,128)(2,1)} %cot.3) | copy-start | bytes 294916
  2.2 0.8 %copy-start.6 = (bf16[96,256]{1,0:T(8,128)(2,1)S(1)}, bf16[96,256]{1,0:T(8,128)(2,1)}, u32[]{:S(2)}) copy-start(bf16[96,256]{1,0:T(8,128)(2,1)} %own_ref.1) | copy-start | bytes 147460
  3.0 13.2 %copy-start.1 = (bf16[3,128,128]{2,1,0:T(8,128)(2,1)S(1)}, bf16[3,128,128]{2,1,0:T(8,128)(2,1)}, u32[]{:S(2)}) copy-start(bf16[3,128,128]{2,1,0:T(8,128)(2,1)} %cot.3) | copy-start | bytes 294916
  3.0 13.2 %copy-start.2 = (bf16[9,64,64]{2,1,0:T(8,128)(2,1)S(1)}, bf16[9,64,64]{2,1,0:T(8,128)(2,1)}, u32[]{:S(2)}) copy-start(bf16[9,64,64]{2,1,0:T(8,128)(2,1)} %k1.1) | copy-start | bytes 221188
  3.0 13.2 %copy-start.3 = (bf16[9,64,64]{2,1,0:T(8,128)(2,1)S(1)}, bf16[9,64,64]{2,1,0:T(8,128)(2,1)}, u32[]{:S(2)}) copy-start(bf16[9,64,64]{2,1,0:T(8,128)(2,1)} %k2.1) | copy-start | bytes 221188
  3.0 13.2 %copy-start.4 = (bf16[256,64]{0,1:T(8,128)(2,1)S(1)}, bf16[256,64]{0,1:T(8,128)(2,1)}, u32[]{:S(2)}) copy-start(bf16[256,64]{0,1:T(8,128)(2,1)} %param.11) | copy-start | bytes 98308
  3.0 13.2 %copy-start.5 = (bf16[256,64]{0,1:T(8,128)(2,1)S(1)}, bf16[256,64]{0,1:T(8,128)(2,1)}, u32[]{:S(2)}) copy-start(bf16[256,64]{0,1:T(8,128)(2,1)} %param.12) | copy-start | bytes 98308
  3.0 13.2 %copy-start.7 = (s32[2]{0:T(128)S(1)}, s32[2]{0:T(128)}, u32[]{:S(2)}) copy-start(s32[2]{0:T(128)} %dil.1) | copy-start | bytes 28
  3.0 13.2 %copy-start.8 = (s32[1,12]{1,0:T(1,128)S(1)}, s32[1,12]{1,0:T(1,128)}, u32[]{:S(2)}) copy-start(s32[1,12]{1,0:T(1,128)} %table.1) | copy-start | bytes 148
  3.0 13.2 %copy-start.9 = (bf16[64]{0:T(256)(128)(2,1)S(1)}, bf16[64]{0:T(256)(128)(2,1)}, u32[]{:S(2)}) copy-start(bf16[64]{0:T(256)(128)(2,1)} %param.15) | copy-start | bytes 388
